TPU v7x, 256 devices: a whole 4x4x8 slice. The times are simulated.
256 devices in a mesh: ctx: 16 (over z, y_lo), exp: 16 (over y_hi, x, core).
Axes of the slice: x: 4, y: 4 (y_hi: 2, y_lo: 2; y = y_hi * 2 + y_lo), z: 8, core: 2. Of those that a mesh axis runs over, the one named last changes fastest.
Arguments:
- queries: bfloat16 [16, 2048, 4096], P('exp', 'ctx'), may hold values from -40 to 40
- keys_values: bfloat16 [16, 2048, 512], P('exp', 'ctx'), may hold values from -24 to 24
- norm_gain: float32 [4096], replicated, may hold values from 0.1 to 1.9
- routing: int32 [16, 2048, 8], P('exp', 'ctx'), may hold values from 0 to 127, all different within a row; in each aligned block of 128 rows (0 to 127, 128 to 255, ..., all dimensions but the last counted through in order) at most 9 rows name the same one
- gate_weights: float32 [16, 2048, 8], P('exp', 'ctx'), may hold values from 0.1 to 1
- expert_in: bfloat16 [256, 512, 2, 1536], P(('exp', 'ctx')), may hold values from -0.09375 to 0.09375
- expert_out: bfloat16 [256, 1536, 512], P(('exp', 'ctx')), may hold values from -0.15625 to 0.15625
Outputs:
- attended: bfloat16 [16, 2048, 4096], P('exp', 'ctx')
- expert_mix: bfloat16 [16, 2048, 4096], P('exp', 'ctx')
Inputs may be any that keep to these rules, and one draw needn't show every extreme that they name: `routing`: each token names 8 different experts; the 128 tokens of one device name one expert at most 9 times.
All inputs are finite; a program needn't handle non-finite values.
Results may differ from a plain program's by a relative error of at most 0.03.
Values may be sent and summed in bfloat16 or wider, within the bound.
A program may use at most 128 MiB of HBM per device.

v0:
```python
import math

import jax
import jax.numpy as jnp
from jax import lax
from jax.sharding import PartitionSpec as P

D = 4096
FF = 1536
HEAD = 128
TOP = 8
QH = 32
KVH = 2
GROUP = 8
CAP = 9


def swapped(array, axis, stride):
    return lax.ppermute(array, axis, [(i, i ^ 1 << stride) for i in range(lax.axis_size(axis))])


def local(queries, keys_values, norm_gain, routing, gate_weights, expert_in, expert_out):
    tok = queries.shape[1]
    share = QH // KVH
    first = lax.axis_index("ctx") * tok
    local_q = queries[0].reshape(tok, KVH, share, HEAD)
    query_place = first + jnp.arange(tok)

    def compute(state, block_rows, start):
        running, total, accum = state
        count = block_rows.shape[0]
        keys = block_rows[:, : KVH * HEAD].reshape(count, KVH, HEAD)
        vals = block_rows[:, KVH * HEAD :].reshape(count, KVH, HEAD)
        scores = jnp.einsum(
            "qkgh,nkh->kgqn", local_q, keys, preferred_element_type=jnp.float32
        ) / math.sqrt(HEAD)
        allowed = (start + jnp.arange(count))[None, :] <= query_place[:, None]
        scores = jnp.where(allowed, scores, -1e30)
        newest = jnp.maximum(running, jnp.max(scores, axis=-1))
        keep = jnp.exp(running - newest)
        weights = jnp.where(allowed, jnp.exp(scores - newest[..., None]), 0.0)
        total = total * keep + jnp.sum(weights, axis=-1)
        accum = accum * keep[..., None] + jnp.einsum(
            "kgqn,nkh->kgqh", weights.astype(jnp.bfloat16), vals, preferred_element_type=jnp.float32
        )
        return (newest, total, accum)

    initial = (
        jnp.full((KVH, share, tok), -1e30, jnp.float32),
        jnp.zeros((KVH, share, tok), jnp.float32),
        jnp.zeros((KVH, share, tok, HEAD), jnp.float32),
    )
    piece = lax.all_gather(keys_values, "ctx", axis=1, tiled=True)
    count = piece.shape[1]
    per = 1
    for factor in (2, 4):
        per = factor
    block = tok * per
    blocks = piece[0].reshape(count // block, block, piece.shape[2])

    def visit(index, kept):
        block_rows = lax.dynamic_index_in_dim(blocks, index, 0, keepdims=False)
        block_start = index * block
        return lax.cond(
            block_start > first + tok - 1,
            lambda inner: inner,
            lambda inner: compute(inner, block_rows, block_start),
            kept,
        )

    running, total, accum = lax.fori_loop(0, count // block, visit, initial)
    attended = (
        (accum / total[..., None])
        .transpose(2, 0, 1, 3)
        .reshape(tok, QH * HEAD)
        .astype(jnp.bfloat16)
    )
    values = attended.astype(jnp.float32)
    normed = (
        values * lax.rsqrt(jnp.mean(values * values, axis=-1, keepdims=True) + 1e-06) * norm_gain
    ).astype(jnp.bfloat16)
    exp_count = lax.axis_size("exp")
    ctx_count = lax.axis_size("ctx")
    experts_here = exp_count * ctx_count // GROUP
    width = D // GROUP
    levels = GROUP.bit_length() - 1
    position = lax.axis_index("ctx")
    routes = routing[0].reshape(-1)
    factors = gate_weights[0].reshape(-1)
    onehot = (routes[:, None] == jnp.arange(experts_here)[None, :]).astype(jnp.int32)
    before = jnp.cumsum(onehot, axis=0) - onehot
    slot = jnp.sum(before * onehot, axis=1)
    valid = routes < experts_here
    target = jnp.where(valid, routes * CAP + slot, experts_here * CAP)
    token_ids = jnp.arange(tok * TOP, dtype=jnp.int32) // TOP
    table = (
        jnp.full((experts_here * CAP + 1,), tok, jnp.int32)
        .at[target]
        .set(token_ids)[: experts_here * CAP]
    )
    padded = jnp.concatenate([normed, jnp.zeros((1, D), jnp.bfloat16)], axis=0)
    outgoing = padded[table].reshape(exp_count, ctx_count // GROUP, CAP, GROUP, width)
    outgoing = outgoing.transpose(0, 1, 3, 2, 4).reshape(exp_count, ctx_count, CAP, width)
    arrived = lax.all_to_all(
        lax.all_to_all(outgoing, "ctx", split_axis=1, concat_axis=1, tiled=True),
        "exp",
        split_axis=0,
        concat_axis=0,
        tiled=True,
    )
    rows = arrived.reshape(-1, width)
    w_in = expert_in[0].reshape(width, 2 * FF)
    w_out = expert_out[0]
    partials = jnp.dot(rows, w_in, preferred_element_type=jnp.float32).astype(jnp.bfloat16)
    current = partials
    for level in range(levels):
        bit = levels - 1 - level
        half = current.shape[0] // 2
        upper = position >> bit & 1
        kept = lax.dynamic_slice_in_dim(current, upper * half, half, 0).astype(jnp.bfloat16)
        sent = lax.dynamic_slice_in_dim(current, (1 - upper) * half, half, 0).astype(jnp.bfloat16)
        received = swapped(sent, "ctx", bit)
        current = lax.optimization_barrier(kept).astype(jnp.float32) + received.astype(jnp.float32)
    hidden = (jax.nn.silu(current[:, :FF]) * current[:, FF:]).astype(jnp.bfloat16)
    for bit in range(levels):
        upper = position >> bit & 1
        other = swapped(hidden, "ctx", bit)
        hidden = jnp.where(
            upper == 1,
            jnp.concatenate([other, hidden], axis=0),
            jnp.concatenate([hidden, other], axis=0),
        )
    produced = jnp.dot(hidden, w_out, preferred_element_type=jnp.float32).astype(jnp.bfloat16)
    returned = lax.all_to_all(
        lax.all_to_all(
            produced.reshape(exp_count, ctx_count, CAP, width),
            "ctx",
            split_axis=1,
            concat_axis=1,
            tiled=True,
        ),
        "exp",
        split_axis=0,
        concat_axis=0,
        tiled=True,
    )
    flat_back = returned.reshape(exp_count, ctx_count // GROUP, GROUP, CAP, width)
    flat_back = flat_back.transpose(0, 1, 3, 2, 4).reshape(experts_here * CAP, D)
    picked = flat_back[jnp.where(valid, target, 0)]
    scale = jnp.where(valid, factors, 0.0)
    mixed = jnp.sum((picked.astype(jnp.float32) * scale[:, None]).reshape(tok, TOP, D), axis=1)
    return (attended[None], mixed.astype(jnp.bfloat16)[None])


def solution(mesh):
    in_specs = (
        P("exp", "ctx", None),
        P("exp", "ctx", None),
        P(),
        P("exp", "ctx", None),
        P("exp", "ctx", None),
        P(("exp", "ctx"), None, None, None),
        P(("exp", "ctx"), None, None),
    )
    out_specs = (P("exp", "ctx", None), P("exp", "ctx", None))
    return jax.shard_map(local, mesh=mesh, in_specs=in_specs, out_specs=out_specs, check_vma=False)
```

profile of v0, /device:TPU:1, one launch (start us, length us, event | category | flops | bytes accessed | tf_op | source)
XLA Modules:
  0.0 1091.1 jit_solution(6950899920495096319)
XLA Ops:
  8.9 2.3 copy.73
  11.2 1.6 copy.75
  12.8 9.0 reduce-window.6
  22.8 4.8 scatter_custom_fusion
  27.7 49.1 %all-gather.2.cloned.1.call-done = bf16[1,2048,512]{2,1,0:T(8,128)(2,1)} async-done(((bf16[1,128,512]{2,1,0:T(8,128)(2,1)}), bf16[1,2048,512]{2,1,0:T(8,128)(2,1)}) %all-gather.2.cloned.1.call-update) | async-done | bytes 2097168 | tf_op jit(solution)/shard_map/all_gather | solution.py:53
  76.8 4.2 copy.74
  80.9 1.6 broadcast_in_dim.58
  82.5 9.9 while.20
  82.5 9.7 conditional.3
  85.3 2.1 fusion.4
  87.5 3.4 multiply_add_fusion
  92.4 2.1 multiply_reduce_fusion
  96.9 1.8 fusion.23
  98.9 3.9 gather_fusion
  102.8 2.7 copy.101
  107.1 79.0 %all_to_all.20 = bf16[16,16,9,512]{3,0,2,1:T(8,128)(2,1)S(1)} all-to-all(bf16[16,16,9,512]{3,0,2,1:T(8,128)(2,1)S(1)} %copy.85), channel_id=1, replica_groups=mesh['ctx'=16,'exp'=16] {'ctx'}, dimensions={1} | all-to-all | bytes 4718592 | tf_op jit(solution)/shard_map/all_to_all | solution.py:105
  186.1 2.7 copy.86
  188.9 18.2 %all-to-all-start.1 = ((bf16[16,16,9,512]{3,1,2,0:T(8,128)(2,1)}), bf16[16,16,9,512]{3,1,2,0:T(8,128)(2,1)}, u32[]{:S(2)}, u32[]{:S(2)}) async-start(bf16[16,16,9,512]{3,1,2,0:T(8,128)(2,1)} %copy.86), calls=%async_computation.1 | async-start | bytes 4718592 | tf_op jit(solution)/shard_map/all_to_all | solution.py:104
  207.1 4.3 copy.102
  211.4 27.2 %all-to-all-done.1 = bf16[16,16,9,512]{3,1,2,0:T(8,128)(2,1)} async-done(((bf16[16,16,9,512]{3,1,2,0:T(8,128)(2,1)}), bf16[16,16,9,512]{3,1,2,0:T(8,128)(2,1)}, u32[]{:S(2)}, u32[]{:S(2)}) %all-to-all-start.1) | async-done | bytes 2359328 | tf_op jit(solution)/shard_map/all_to_all | solution.py:104
  238.6 5.5 copy.87
  244.1 5.6 reshape.178
  249.7 9.9 convolution_convert_fusion
  259.5 5.4 constant_dynamic-slice_fusion.1
  265.5 306.4 %collective-permute-done = bf16[1152,3072]{1,0:T(8,128)(2,1)} collective-permute-done((bf16[1152,3072]{1,0:T(8,128)(2,1)}, bf16[1152,3072]{1,0:T(8,128)(2,1)}, u32[]{:S(2)}, u32[]{:S(2)}) %collective-permute-start) | collective-permute-done | bytes 7077920 | tf_op jit(solution)/shard_map/ppermute | solution.py:19
  572.0 11.2 %convert_add_fusion = bf16[1152,3072]{1,0:T(8,128)(2,1)} fusion(bf16[1152,3072]{1,0:T(8,128)(2,1)} %collective-permute-done, bf16[1152,3072]{1,0:T(8,128)(2,1)} %get-tuple-element.379), kind=kLoop, calls=%fused_computation.24 | loop fusion | flops 14155776 | bytes 21233664 | tf_op jit(solution)/shard_map/add | solution.py:123
  583.1 6.6 dynamic-slice_convert_fusion.1
  589.7 77.9 %collective-permute-done.1 = bf16[576,3072]{1,0:T(8,128)(2,1)} collective-permute-done((bf16[576,3072]{1,0:T(8,128)(2,1)}, bf16[576,3072]{1,0:T(8,128)(2,1)}, u32[]{:S(2)}, u32[]{:S(2)}) %collective-permute-start.1) | collective-permute-done | bytes 3538976 | tf_op jit(solution)/shard_map/ppermute | solution.py:19
  667.6 4.4 convert_add_fusion.1
  672.4 38.7 %collective-permute-done.2 = bf16[288,3072]{1,0:T(8,128)(2,1)S(1)} collective-permute-done((bf16[288,3072]{1,0:T(8,128)(2,1)S(1)}, bf16[288,3072]{1,0:T(8,128)(2,1)S(1)}, u32[]{:S(2)}, u32[]{:S(2)}) %collective-permute-start.2) | collective-permute-done | bytes 1769504 | tf_op jit(solution)/shard_map/ppermute | solution.py:19
  713.2 18.2 %collective-permute-done.3 = bf16[288,1536]{1,0:T(8,128)(2,1)} collective-permute-done((bf16[288,1536]{1,0:T(8,128)(2,1)S(1)}, bf16[288,1536]{1,0:T(8,128)(2,1)}, u32[]{:S(2)}, u32[]{:S(2)}) %collective-permute-start.3) | collective-permute-done | bytes 884768 | tf_op jit(solution)/shard_map/ppermute | solution.py:19
  731.4 2.5 maximum_select_fusion.5
  734.9 36.1 %collective-permute-done.4 = bf16[576,1536]{1,0:T(8,128)(2,1)} collective-permute-done((bf16[576,1536]{1,0:T(8,128)(2,1)S(1)}, bf16[576,1536]{1,0:T(8,128)(2,1)}, u32[]{:S(2)}, u32[]{:S(2)}) %collective-permute-start.4) | collective-permute-done | bytes 1769504 | tf_op jit(solution)/shard_map/ppermute | solution.py:19
  770.9 3.8 maximum_select_fusion.4
  775.1 154.4 %collective-permute-done.5 = bf16[1152,1536]{1,0:T(8,128)(2,1)} collective-permute-done((bf16[1152,1536]{1,0:T(8,128)(2,1)}, bf16[1152,1536]{1,0:T(8,128)(2,1)}, u32[]{:S(2)}, u32[]{:S(2)}) %collective-permute-start.5) | collective-permute-done | bytes 3538976 | tf_op jit(solution)/shard_map/ppermute | solution.py:19
  929.5 9.5 fusion.21
  939.0 5.3 reshape.179
  944.4 3.9 copy.88
  948.3 58.7 %all_to_all.21 = bf16[16,16,9,512]{3,0,2,1:T(8,128)(2,1)S(1)} all-to-all(bf16[16,16,9,512]{3,0,2,1:T(8,128)(2,1)S(1)} %copy.88), channel_id=1, replica_groups=mesh['ctx'=16,'exp'=16] {'ctx'}, dimensions={1} | all-to-all | bytes 4718592 | tf_op jit(solution)/shard_map/all_to_all | solution.py:135
  1007.0 2.7 copy.89
  1009.7 8.4 all-to-all-start.3
  1018.2 1.6 copy.76
  1019.8 2.3 convert_element_type.116
  1022.1 27.4 %all-to-all-done.3 = bf16[16,16,9,512]{3,1,2,0:T(8,128)(2,1)} async-done(((bf16[16,16,9,512]{3,1,2,0:T(8,128)(2,1)}), bf16[16,16,9,512]{3,1,2,0:T(8,128)(2,1)}, u32[]{:S(2)}, u32[]{:S(2)}) %all-to-all-start.3) | async-done | bytes 2359328 | tf_op jit(solution)/shard_map/all_to_all | solution.py:134
  1049.6 1.8 copy.90
  1051.4 2.5 copy.103
  1053.9 17.2 %gather_fusion.1 = bf16[1024,4096]{1,0:T(8,128)(2,1)} fusion(bf16[288,4096]{1,0:T(8,128)(2,1)} %bitcast.92, s32[1024]{0:T(1024)S(1)} %broadcast_clamp_fusion), kind=kCustom, calls=%fused_computation.1 | custom fusion | bytes 16781312 | tf_op jit(solution)/shard_map/gather | solution.py:149
  1071.2 12.9 %fusion.13 = bf16[128,4096]{1,0:T(8,128)(2,1)} fusion(bf16[1024,4096]{1,0:T(8,128)(2,1)} %gather_fusion.1, f32[128,8]{1,0:T(8,128)S(1)} %copy.91), kind=kLoop, calls=%fused_computation.23 | loop fusion | flops 12058624 | bytes 9441280 | tf_op jit(solution)/shard_map/reduce_sum | solution.py:151
  (82 shorter events, 15.5 us)
Async XLA Ops:
  7.2 922.4 %copy-start = (bf16[1,1536,512]{2,1,0:T(8,128)(2,1)S(1)}, bf16[1,1536,512]{2,1,0:T(8,128)(2,1)}, u32[]{:S(2)}) copy-start(bf16[1,1536,512]{2,1,0:T(8,128)(2,1)} %param.17) | copy-start | bytes 4718596
  7.2 15.0 %copy-start.6 = (s32[1,128,8]{1,2,0:T(8,128)S(1)}, s32[1,128,8]{1,2,0:T(8,128)}, u32[]{:S(2)}) copy-start(s32[1,128,8]{1,2,0:T(8,128)} %param.14) | copy-start | bytes 12292
  7.2 15.0 %copy-start.8 = (f32[1,128,8]{1,2,0:T(8,128)S(1)}, f32[1,128,8]{1,2,0:T(8,128)}, u32[]{:S(2)}) copy-start(f32[1,128,8]{1,2,0:T(8,128)} %param.15) | copy-start | bytes 12292
  7.2 69.6 %all-gather.2.cloned.1.call-start = ((), (), s32[]{:S(2)}) async-start(), calls=%async_computation.4 | async-start | bytes 2228224 | tf_op jit(solution)/shard_map/all_gather | solution.py:53
  85.3 2.2 copy-start.3
  90.9 1.3 copy-start.4
  94.5 1.0 copy-start.1
  95.5 1.5 copy-start.7
  188.9 49.7 %all-to-all-start.1 = ((bf16[16,16,9,512]{3,1,2,0:T(8,128)(2,1)}), bf16[16,16,9,512]{3,1,2,0:T(8,128)(2,1)}, u32[]{:S(2)}, u32[]{:S(2)}) async-start(bf16[16,16,9,512]{3,1,2,0:T(8,128)(2,1)} %copy.86), calls=%async_computation.1 | async-start | bytes 4718592 | tf_op jit(solution)/shard_map/all_to_all | solution.py:104
  264.9 307.1 %collective-permute-start = (bf16[1152,3072]{1,0:T(8,128)(2,1)}, bf16[1152,3072]{1,0:T(8,128)(2,1)}, u32[]{:S(2)}, u32[]{:S(2)}) collective-permute-start(bf16[1152,3072]{1,0:T(8,128)(2,1)} %get-tuple-element.380), channel_id=1, source_target_pairs={{0,64},{16,80},{32,96},{48,112},{64,0},{80,16},{96,32},{112,48},{1... | collective-permute-start | bytes 21233672 | tf_op jit(solution)/shard_map/ppermute | solution.py:19
  589.7 77.9 %collective-permute-start.1 = (bf16[576,3072]{1,0:T(8,128)(2,1)}, bf16[576,3072]{1,0:T(8,128)(2,1)}, u32[]{:S(2)}, u32[]{:S(2)}) collective-permute-start(bf16[576,3072]{1,0:T(8,128)(2,1)} %get-tuple-element.382), channel_id=1, source_target_pairs={{0,32},{16,48},{32,0},{48,16},{64,96},{80,112},{96,64},{112,80},{1... | collective-permute-start | bytes 10616840 | tf_op jit(solution)/shard_map/ppermute | solution.py:19
  672.3 38.8 %collective-permute-start.2 = (bf16[288,3072]{1,0:T(8,128)(2,1)S(1)}, bf16[288,3072]{1,0:T(8,128)(2,1)S(1)}, u32[]{:S(2)}, u32[]{:S(2)}) collective-permute-start(bf16[288,3072]{1,0:T(8,128)(2,1)S(1)} %get-tuple-element.384), channel_id=1, source_target_pairs={{0,16},{16,0},{32,48},{48,32},{64,80},{80,64},{96,112},{112,96},{1... | collective-permute-start | bytes 5308424 | tf_op jit(solution)/shard_map/ppermute | solution.py:19
  712.3 0.9 copy-start.5
  712.3 19.1 %collective-permute-start.3 = (bf16[288,1536]{1,0:T(8,128)(2,1)S(1)}, bf16[288,1536]{1,0:T(8,128)(2,1)}, u32[]{:S(2)}, u32[]{:S(2)}) collective-permute-start(bf16[288,1536]{1,0:T(8,128)(2,1)S(1)} %fusion.24), channel_id=1, source_target_pairs={{0,16},{16,0},{32,48},{48,32},{64,80},{80,64},{96,112},{112,96},{1... | collective-permute-start | bytes 2654216 | tf_op jit(solution)/shard_map/ppermute | solution.py:19
  733.8 37.1 %collective-permute-start.4 = (bf16[576,1536]{1,0:T(8,128)(2,1)S(1)}, bf16[576,1536]{1,0:T(8,128)(2,1)}, u32[]{:S(2)}, u32[]{:S(2)}) collective-permute-start(bf16[576,1536]{1,0:T(8,128)(2,1)S(1)} %maximum_select_fusion.5), channel_id=1, source_target_pairs={{0,32},{16,48},{32,0},{48,16},{64,96},{80,112},{96,64},{112,80},{1... | collective-permute-start | bytes 5308424 | tf_op jit(solution)/shard_map/ppermute | solution.py:19
  774.7 154.8 %collective-permute-start.5 = (bf16[1152,1536]{1,0:T(8,128)(2,1)}, bf16[1152,1536]{1,0:T(8,128)(2,1)}, u32[]{:S(2)}, u32[]{:S(2)}) collective-permute-start(bf16[1152,1536]{1,0:T(8,128)(2,1)} %maximum_select_fusion.4), channel_id=1, source_target_pairs={{0,64},{16,80},{32,96},{48,112},{64,0},{80,16},{96,32},{112,48},{1... | collective-permute-start | bytes 10616840 | tf_op jit(solution)/shard_map/ppermute | solution.py:19
  1009.7 8.5 copy-start.2
  1009.7 39.9 %all-to-all-start.3 = ((bf16[16,16,9,512]{3,1,2,0:T(8,128)(2,1)}), bf16[16,16,9,512]{3,1,2,0:T(8,128)(2,1)}, u32[]{:S(2)}, u32[]{:S(2)}) async-start(bf16[16,16,9,512]{3,1,2,0:T(8,128)(2,1)} %copy.89), calls=%async_computation.3 | async-start | bytes 4718592 | tf_op jit(solution)/shard_map/all_to_all | solution.py:134
Sparse Core Ops, SparseCore 0:
  9.8 66.9 all-gather.1
where the time goes:
time: 1090 us
  waiting for transfers between devices  736 us (68%)
  blocking collectives  138 us (13%)
  local copies, waits for them, and re-layouts  97.7 us (9%)
  other arithmetic  51.6 us (5%)
  starting transfers between devices  28.9 us (3%)
  matrix products  24.2 us (2%)
  between operations  14.6 us (1%)
    ppermute x6, waiting for transfers between devices, swapped(): lax.ppermute(array, axis, [(i, i ^ 1 << stride) for i in range(lax.axis_s...  632 us
    all_to_all x1, blocking collectives, local(): lax.all_to_all(outgoing, 'ctx', split_axis=1, concat_axis=1, tiled=True)  79 us
    all_to_all x1, blocking collectives, local(): lax.all_to_all(produced.reshape(exp_count, ctx_count, CAP, width), 'ctx',...  58.7 us
    all_gather x1, waiting for transfers between devices, local(): piece = lax.all_gather(keys_values, 'ctx', axis=1, tiled=True)  49.1 us
    all_to_all x1, waiting for transfers between devices, local(): lax.all_to_all(lax.all_to_all(produced.reshape(exp_count, ctx_count, CAP,...  27.4 us
    all_to_all x1, waiting for transfers between devices, local(): lax.all_to_all(lax.all_to_all(outgoing, 'ctx', split_axis=1, concat_axis=...  27.2 us
  transfers between devices with their start and end apart: 9, of which 9 were waited for; matrix products, arithmetic and copies ran while one was open for 3% of the time, Pallas kernels for 0%

commit v1 on v0

v1 whole, which is shorter than its diff:
```python
import functools
import math

import jax
import jax.numpy as jnp
from jax import lax
from jax.experimental import pallas as pl
from jax.experimental.pallas import tpu as pltpu
from jax.sharding import PartitionSpec as P

D = 4096
FF = 1536
HEAD = 128
TOP = 8
QH = 32
KVH = 2
GROUP = 8
CAP = 9
EXPERTS = 32
N_EXP = 16
N_Z = 8
ROWS = N_EXP * N_Z * CAP
HALF = ROWS // 2
CHUNK = 32
COUNT = HALF // CHUNK
PACK = 3
BLOCK = CHUNK * PACK
LAG = 2
TILE = 512
PART = D // 4
STRIPE = D // GROUP


def expert_kernel(x_ref, in_own, in_oth, out_own, out_oth, y_ref, part, recv, hid, s_send, s_recv, h_send, h_recv):
    c = lax.axis_index("ctx")
    side = c % 2
    place = (c // 2) % 4

    barrier = pltpu.get_barrier_semaphore()

    @pl.when(place > 0)
    def _():
        pl.semaphore_signal(barrier, inc=1, device_id={"ctx": c - 2}, device_id_type=pl.DeviceIdType.MESH)

    @pl.when(place < 3)
    def _():
        pl.semaphore_signal(barrier, inc=1, device_id={"ctx": c + 2}, device_id_type=pl.DeviceIdType.MESH)

    pl.semaphore_wait(barrier, jnp.where((place > 0) & (place < 3), 2, 1))

    own = pl.ds(pl.multiple_of(side * STRIPE, STRIPE), STRIPE)
    oth = pl.ds(pl.multiple_of((1 - side) * STRIPE, STRIPE), STRIPE)

    def sum_copy(d, i):
        target = jnp.where(d == 1, c + 2, c - 2)
        return pltpu.make_async_remote_copy(
            src_ref=part.at[d, i], dst_ref=recv.at[d, i], send_sem=s_send.at[d, i], recv_sem=s_recv.at[d, i],
            device_id={"ctx": target}, device_id_type=pl.DeviceIdType.MESH)

    def hid_copy(d, i):
        target = jnp.where(d == 1, c - 2, c + 2)
        return pltpu.make_async_remote_copy(
            src_ref=hid.at[d, i], dst_ref=hid.at[d, i], send_sem=h_send.at[d, i], recv_sem=h_recv.at[d, i],
            device_id={"ctx": target}, device_id_type=pl.DeviceIdType.MESH)

    def products(d, b):
        def tile(n, _):
            cols = pl.ds(pl.multiple_of(n * TILE, TILE), TILE)
            acc = jnp.dot(x_ref[d, b, :, own], in_own[:, cols], preferred_element_type=jnp.float32)
            acc += jnp.dot(x_ref[d, b, :, oth], in_oth[:, cols], preferred_element_type=jnp.float32)
            part[d, pl.ds(b * PACK, PACK), :, cols] = acc.astype(jnp.bfloat16).reshape(PACK, CHUNK, TILE)
            return 0
        lax.fori_loop(0, 2 * FF // TILE, tile, 0)

    def result(d, b):
        rows = hid[d, pl.ds(b * PACK, PACK)].reshape(BLOCK, FF)
        y_ref[d, b, :, own] = jnp.dot(rows, out_own[...], preferred_element_type=jnp.float32).astype(jnp.bfloat16)
        y_ref[d, b, :, oth] = jnp.dot(rows, out_oth[...], preferred_element_type=jnp.float32).astype(jnp.bfloat16)

    def step(t, _):
        @pl.when((t % PACK == 0) & (t < COUNT))
        def _():
            def both(d, _):
                products(d, t // PACK)
                return 0
            lax.fori_loop(0, 2, both, 0)

        def direction(d, _):
            pos = jnp.where(d == 1, place, 3 - place)
            i = t - LAG * pos

            @pl.when((i >= 0) & (i < COUNT))
            def _():
                @pl.when(pos == 0)
                def _():
                    sum_copy(d, i).start()

                @pl.when((pos > 0) & (pos < 3))
                def _():
                    sum_copy(d, i).wait_recv()
                    part[d, i] = (part[d, i].astype(jnp.float32) + recv[d, i].astype(jnp.float32)).astype(jnp.bfloat16)
                    sum_copy(d, i).start()

                @pl.when(pos == 3)
                def _():
                    sum_copy(d, i).wait_recv()
                    total = part[d, i].astype(jnp.float32) + recv[d, i].astype(jnp.float32)
                    gate = total[:, :FF]
                    hid[d, i] = (jax.nn.silu(gate) * total[:, FF:]).astype(jnp.bfloat16)
                    hid_copy(d, i).start()

            k = t - 3 * LAG - LAG * (3 - pos)

            @pl.when((k >= 0) & (k < COUNT))
            def _():
                @pl.when(pos < 3)
                def _():
                    hid_copy(d, k).wait_recv()

                @pl.when((pos > 0) & (pos < 3))
                def _():
                    hid_copy(d, k).start()

                @pl.when(k % PACK == PACK - 1)
                def _():
                    result(d, k // PACK)
            return 0

        lax.fori_loop(0, 2, direction, 0)
        return 0

    lax.fori_loop(0, COUNT + 6 * LAG, step, 0)

    def drain(i, _):
        def direction(d, _):
            pos = jnp.where(d == 1, place, 3 - place)

            @pl.when(pos < 3)
            def _():
                sum_copy(d, i).wait_send()

            @pl.when(pos > 0)
            def _():
                hid_copy(d, i).wait_send()
            return 0
        lax.fori_loop(0, 2, direction, 0)
        return 0

    lax.fori_loop(0, COUNT, drain, 0)


def experts(rows, in_own, in_oth, out_own, out_oth):
    vmem = pl.BlockSpec(memory_space=pltpu.VMEM)
    return pl.pallas_call(
        expert_kernel,
        out_shape=jax.ShapeDtypeStruct((2, COUNT // PACK, BLOCK, PART), jnp.bfloat16),
        in_specs=[vmem] * 5,
        out_specs=vmem,
        scratch_shapes=[
            pltpu.VMEM((2, COUNT, CHUNK, 2 * FF), jnp.bfloat16),
            pltpu.VMEM((2, COUNT, CHUNK, 2 * FF), jnp.bfloat16),
            pltpu.VMEM((2, COUNT, CHUNK, FF), jnp.bfloat16),
            pltpu.SemaphoreType.DMA((2, COUNT)),
            pltpu.SemaphoreType.DMA((2, COUNT)),
            pltpu.SemaphoreType.DMA((2, COUNT)),
            pltpu.SemaphoreType.DMA((2, COUNT)),
        ],
        compiler_params=pltpu.CompilerParams(collective_id=3, has_side_effects=True, vmem_limit_bytes=48 * 2**20),
        cost_estimate=pl.CostEstimate(flops=2 * ROWS * (PART * 2 * FF + FF * PART), bytes_accessed=14 * 2**20, transcendentals=HALF * FF),
        name="experts",
    )(rows.reshape(2, COUNT // PACK, BLOCK, PART), in_own, in_oth, out_own, out_oth).reshape(ROWS, PART)


def paired(array):
    return lax.ppermute(array, "ctx", [(i, i ^ 1) for i in range(16)])


def along_z(array):
    groups = [[2 * z + side for z in range(N_Z)] for side in range(2)]
    return lax.all_to_all(array, "ctx", split_axis=0, concat_axis=0, axis_index_groups=groups, tiled=True)


def along_exp(array):
    return lax.all_to_all(array, "exp", split_axis=0, concat_axis=0, tiled=True)


def attention(queries, keys_values):
    tok = queries.shape[1]
    share = QH // KVH
    first = lax.axis_index("ctx") * tok
    local_q = queries[0].reshape(tok, KVH, share, HEAD)
    query_place = first + jnp.arange(tok)

    def compute(state, block_rows, start):
        running, total, accum = state
        count = block_rows.shape[0]
        keys = block_rows[:, : KVH * HEAD].reshape(count, KVH, HEAD)
        vals = block_rows[:, KVH * HEAD :].reshape(count, KVH, HEAD)
        scores = jnp.einsum(
            "qkgh,nkh->kgqn", local_q, keys, preferred_element_type=jnp.float32
        ) / math.sqrt(HEAD)
        allowed = (start + jnp.arange(count))[None, :] <= query_place[:, None]
        scores = jnp.where(allowed, scores, -1e30)
        newest = jnp.maximum(running, jnp.max(scores, axis=-1))
        keep = jnp.exp(running - newest)
        weights = jnp.where(allowed, jnp.exp(scores - newest[..., None]), 0.0)
        total = total * keep + jnp.sum(weights, axis=-1)
        accum = accum * keep[..., None] + jnp.einsum(
            "kgqn,nkh->kgqh", weights.astype(jnp.bfloat16), vals, preferred_element_type=jnp.float32
        )
        return (newest, total, accum)

    initial = (
        jnp.full((KVH, share, tok), -1e30, jnp.float32),
        jnp.zeros((KVH, share, tok), jnp.float32),
        jnp.zeros((KVH, share, tok, HEAD), jnp.float32),
    )
    piece = lax.all_gather(keys_values, "ctx", axis=1, tiled=True)
    count = piece.shape[1]
    block = tok * 4
    blocks = piece[0].reshape(count // block, block, piece.shape[2])

    def visit(index, kept):
        block_rows = lax.dynamic_index_in_dim(blocks, index, 0, keepdims=False)
        block_start = index * block
        return lax.cond(
            block_start > first + tok - 1,
            lambda inner: inner,
            lambda inner: compute(inner, block_rows, block_start),
            kept,
        )

    running, total, accum = lax.fori_loop(0, count // block, visit, initial)
    return (
        (accum / total[..., None])
        .transpose(2, 0, 1, 3)
        .reshape(tok, QH * HEAD)
        .astype(jnp.bfloat16)
    )


def local(queries, keys_values, norm_gain, routing, gate_weights, expert_in, expert_out):
    tok = queries.shape[1]
    in_own = expert_in[0].reshape(STRIPE, 2 * FF)
    out_own = expert_out[0]
    in_oth = paired(in_own)
    out_oth = paired(out_own)

    same = routing[0][:, :, None] == jnp.arange(EXPERTS)[None, None, :]
    gates = jnp.sum(jnp.where(same, gate_weights[0][:, :, None], 0.0), axis=1)
    hit = jnp.any(same, axis=1)
    earlier = jnp.arange(tok)[:, None] > jnp.arange(tok)[None, :]
    slot = jnp.dot(earlier.astype(jnp.bfloat16), hit.astype(jnp.bfloat16), preferred_element_type=jnp.float32)
    chosen = hit[:, :, None] & (slot[:, :, None] == jnp.arange(CAP, dtype=jnp.float32)[None, None, :])
    chosen = chosen.reshape(tok, N_EXP, 2, CAP).transpose(0, 2, 1, 3)
    spread = jnp.where(chosen, gates.reshape(tok, N_EXP, 2, 1).transpose(0, 2, 1, 3), 0.0).reshape(tok, EXPERTS * CAP)
    pick = chosen.reshape(tok, EXPERTS * CAP).astype(jnp.bfloat16)
    high = lax.reduce_precision(spread, 8, 7)
    low = spread - high
    spread = jnp.concatenate([high, low], axis=0).astype(jnp.bfloat16)

    attended = attention(queries, keys_values)
    values = attended.astype(jnp.float32)
    normed = (
        values * lax.rsqrt(jnp.mean(values * values, axis=-1, keepdims=True) + 1e-06) * norm_gain
    ).astype(jnp.bfloat16)

    outgoing = lax.dot_general(pick, normed, (((0,), (0,)), ((), ())), preferred_element_type=jnp.float32)
    outgoing = outgoing.astype(jnp.bfloat16).reshape(2, N_EXP * CAP, 4, PART).transpose(0, 2, 1, 3)
    middle = along_z(outgoing.reshape(N_Z, N_EXP * CAP, PART))
    middle = middle.reshape(N_Z, N_EXP, CAP, PART).transpose(1, 0, 2, 3)
    rows = along_exp(middle.reshape(N_EXP, N_Z * CAP, PART)).reshape(ROWS, PART)

    made = experts(rows, in_own, in_oth, out_own, out_oth)

    middle = along_exp(made.reshape(N_EXP, N_Z * CAP, PART))
    middle = middle.reshape(N_EXP, N_Z, CAP, PART).transpose(1, 0, 2, 3)
    back = along_z(middle.reshape(N_Z, N_EXP * CAP, PART))
    back = back.reshape(2, 4, N_EXP * CAP, PART).transpose(0, 2, 1, 3).reshape(EXPERTS * CAP, D)
    mixed = jnp.dot(spread, back, preferred_element_type=jnp.float32)
    mixed = mixed[:tok] + mixed[tok:]
    return (attended[None], mixed.astype(jnp.bfloat16)[None])


def solution(mesh):
    in_specs = (
        P("exp", "ctx", None),
        P("exp", "ctx", None),
        P(),
        P("exp", "ctx", None),
        P("exp", "ctx", None),
        P(("exp", "ctx"), None, None, None),
        P(("exp", "ctx"), None, None),
    )
    out_specs = (P("exp", "ctx", None), P("exp", "ctx", None))
    return jax.shard_map(local, mesh=mesh, in_specs=in_specs, out_specs=out_specs, check_vma=False)
```

time: 1090 us -> 525 us (0.48)
  waiting for transfers between devices: 736 us -> 214 us
  Pallas kernels: 0 us -> 137 us
  blocking collectives: 138 us -> 50.4 us
  local copies, waits for them, and re-layouts: 97.7 us -> 45.2 us
  other arithmetic: 51.6 us -> 7.3 us
  starting transfers between devices: 28.9 us -> 48 us
  matrix products: 24.2 us -> 7.02 us
    ppermute x6 -> x2, waiting for transfers between devices: 632 us -> 60.2 us  [paired(): return lax.ppermute(array, 'ctx', [(i, i ^ 1) for i in range(16)])]
    pallas_call x0 -> x1, Pallas kernels: none -> 137 us  [experts(): pl.pallas_call(expert_kernel, out_shape=jax.ShapeDtypeStruct((2, COUNT //...]
    all_to_all x2 -> x1, blocking collectives: 138 us -> 50.4 us  [along_exp(): return lax.all_to_all(array, 'exp', split_axis=0, concat_axis=0, tiled=True)]
    all_to_all x2 -> x3, waiting for transfers between devices: 54.6 us -> 86.5 us  [the longest x2 86.5 us: along_z(): lax.all_to_all(array, 'ctx', split_axis=0, concat_axis=0, axis_index_grou...]
    gather x2 -> x0, local copies, waits for them, and re-layouts: 21.1 us -> none  [the longest x1 17.2 us: local(): picked = flat_back[jnp.where(valid, target, 0)]]
    all_to_all x2 -> x3, starting transfers between devices: 26.6 us -> 47.1 us  [the longest x2 32.2 us: along_z(): lax.all_to_all(array, 'ctx', split_axis=0, concat_axis=0, axis_index_grou...]
    all_gather x1, waiting for transfers between devices: 49.1 us -> 66.8 us  [attention(): piece = lax.all_gather(keys_values, 'ctx', axis=1, tiled=True)]
    dot_general x2 -> x3, matrix products: 19.4 us -> 2.19 us  [the longest x1 1.28 us: local(): mixed = jnp.dot(spread, back, preferred_element_type=jnp.float32)]
  transfers between devices with their start and end apart: 9 -> 6, of which waited for: 9 -> 4; matrix products, arithmetic and copies ran while one was open for 3% -> 5% of each run, Pallas kernels for 0% -> 0%
where the time goes in v1:
time: 525 us; the launch traced here: 524 us
  waiting for transfers between devices  214 us (41%)
  Pallas kernels  137 us (26%)
  blocking collectives  50.4 us (10%)
  starting transfers between devices  48 us (9%)
  local copies, waits for them, and re-layouts  45.2 us (9%)
  between operations  14.3 us (3%)
  other arithmetic  7.3 us (1%)
  matrix products  7.02 us (1%)
    pallas_call x1, Pallas kernels, experts(): pl.pallas_call(expert_kernel, out_shape=jax.ShapeDtypeStruct((2, COUNT //...  137 us
    all_to_all x2, waiting for transfers between devices, along_z(): lax.all_to_all(array, 'ctx', split_axis=0, concat_axis=0, axis_index_grou...  86.5 us
    all_gather x1, waiting for transfers between devices, attention(): piece = lax.all_gather(keys_values, 'ctx', axis=1, tiled=True)  66.8 us
    ppermute x2, waiting for transfers between devices, paired(): return lax.ppermute(array, 'ctx', [(i, i ^ 1) for i in range(16)])  60.2 us
    all_to_all x1, blocking collectives, along_exp(): return lax.all_to_all(array, 'exp', split_axis=0, concat_axis=0, tiled=True)  50.4 us
    all_to_all x2, starting transfers between devices, along_z(): lax.all_to_all(array, 'ctx', split_axis=0, concat_axis=0, axis_index_grou...  32.2 us
    all_to_all x1, starting transfers between devices, along_exp(): return lax.all_to_all(array, 'exp', split_axis=0, concat_axis=0, tiled=True)  14.9 us
    unnamed x22, local copies, waits for them, and re-layouts  11.9 us
  transfers between devices with their start and end apart: 6, of which 4 were waited for; matrix products, arithmetic and copies ran while one was open for 5% of the time, Pallas kernels for 0%

profile of v1, /device:TPU:1, one launch (start us, length us, event | category | flops | bytes accessed | tf_op | source)
XLA Modules:
  0.0 523.5 jit_solution(7279514102358312371)
XLA Ops:
  7.2 0.7 all-gather.2.cloned.1.call-update
  7.9 1.6 copy.78
  9.5 0.7 copy.80
  10.6 66.8 %all-gather.2.cloned.1.call-done = bf16[1,2048,512]{2,1,0:T(8,128)(2,1)} async-done(((bf16[1,128,512]{2,1,0:T(8,128)(2,1)}), bf16[1,2048,512]{2,1,0:T(8,128)(2,1)}) %all-gather.2.cloned.1.call-update) | async-done | bytes 2097168 | tf_op jit(solution)/shard_map/all_gather | solution.py:218
  77.4 2.8 copy.79
  80.2 1.6 broadcast_in_dim.76
  81.8 8.9 %while.20 = (s32[]{:T(128)}, f32[2,16,128]{2,1,0:T(8,128)S(1)}, f32[2,16,128]{2,1,0:T(8,128)S(1)}, f32[2,16,128,128]{3,2,1,0:T(8,128)}, s32[]{:T(128)}, /*index=...) while((s32[]{:T(128)}, f32[2,16,128]{2,1,0:T(8,128)S(1)}, ...), condition=%wide.region_5.6_spmd.clone, body=%wide.region_0.5_spmd.clone.sunk | while | flops 1102127744 | bytes 50338136 | solution.py:233
  81.8 8.7 %conditional.3 = (f32[2,16,128]{2,1,0:T(8,128)S(1)}, f32[2,16,128]{2,1,0:T(8,128)S(1)}, f32[2,16,128,128]{3,2,1,0:T(8,128)}) conditional(s32[]{:T(128)} %convert_element_type.85, (s32[]{:T(128)}, s32[]{:T(128)}, s32[]{:T(128)}, bf16[4,512,512]{1,2,0:T(8,128)(2,1)S(1)}, bf16[128,2,16,128]{3,0,2,1:T(8,128)(2,1)S(1)}, ...), branch_computations={%region_1.0_spmd, %region_4.4_spmd} | conditional | flops 1102127744 | bytes 50304636 | solution.py:226
  82.0 1.4 fusion.2
  83.5 2.1 fusion.4
  85.7 3.4 multiply_add_fusion
  89.1 1.3 copy-done.4
  90.6 1.9 copy.81
  93.3 0.7 fusion.15
  94.1 0.8 convolution_convert_fusion
  94.9 3.0 reshape.125
  97.9 3.9 copy.85
  101.8 28.2 %all-to-all-start = ((bf16[8,144,1024]{2,1,0:T(8,128)(2,1)}), bf16[8,144,1024]{2,1,0:T(8,128)(2,1)S(1)}, u32[]{:S(2)}, u32[]{:S(2)}) async-start(bf16[8,144,1024]{2,1,0:T(8,128)(2,1)} %bitcast.95), calls=%async_computation | async-start | bytes 4718592 | tf_op jit(solution)/shard_map/all_to_all | solution.py:180
  130.0 4.3 copy.101
  134.3 0.8 collective-permute-start
  135.1 44.6 %all-to-all-done = bf16[8,144,1024]{2,1,0:T(8,128)(2,1)S(1)} async-done(((bf16[8,144,1024]{2,1,0:T(8,128)(2,1)}), bf16[8,144,1024]{2,1,0:T(8,128)(2,1)S(1)}, u32[]{:S(2)}, u32[]{:S(2)}) %all-to-all-start) | async-done | bytes 2359328 | tf_op jit(solution)/shard_map/all_to_all | solution.py:180
  179.7 1.3 copy.86
  181.0 1.3 copy.87
  182.3 2.7 copy.88
  185.0 14.9 %all-to-all-start.1 = ((bf16[16,72,1024]{2,1,0:T(8,128)(2,1)}), bf16[16,72,1024]{2,1,0:T(8,128)(2,1)}, u32[]{:S(2)}, u32[]{:S(2)}) async-start(bf16[16,72,1024]{2,1,0:T(8,128)(2,1)} %copy.88), calls=%async_computation.1 | async-start | bytes 4718592 | tf_op jit(solution)/shard_map/all_to_all | solution.py:184
  200.0 60.2 %collective-permute-done.1.out_oth = bf16[1536,512]{1,0:T(8,128)(2,1)S(1)} collective-permute-done((bf16[1536,512]{1,0:T(8,128)(2,1)S(1)}, bf16[1536,512]{1,0:T(8,128)(2,1)S(1)}, u32[]{:S(2)}, u32[]{:S(2)}) %collective-permute-start.1) | collective-permute-done | bytes 1572896 | tf_op jit(solution)/shard_map/ppermute | solution.py:175
  260.2 136.9 %experts.1 = bf16[2,6,96,1024]{3,2,1,0:T(8,128)(2,1)S(1)} custom-call(bf16[2,6,96,1024]{3,2,1,0:T(8,128)(2,1)} %bitcast.27.x_ref, bf16[512,3072]{1,0:T(8,128)(2,1)} %bitcast.56.in_own, bf16[512,3072]{1,0:T(8,128)(2,1)} %collective-permute-done.in_oth, bf16[1536,512]{1,0:T(8,128)(2,1)S(1)} %bitcast.90, bf16[1536,512]{1,0:T(8,128)(2,1)S(1)} %collective-permute-done.1.out_oth), custom_call_target="tpu_custom_call" | custom-call | flops 10871635968 | bytes 14680064 | tf_op jit(solution)/shard_map/experts/pallas_call | solution.py:154
  397.1 50.4 %all_to_all.20 = bf16[16,72,1024]{2,1,0:T(8,128)(2,1)S(1)} all-to-all(bf16[16,72,1024]{2,1,0:T(8,128)(2,1)S(1)} %bitcast.88), channel_id=1, replica_groups=mesh['ctx'=16,'exp'=16] {'exp'}, dimensions={0} | all-to-all | bytes 4718592 | tf_op jit(solution)/shard_map/all_to_all | solution.py:184
  447.5 1.3 copy.89
  448.8 1.3 copy.90
  450.1 2.7 copy.91
  452.8 4.0 all-to-all-start.3
  456.8 0.7 eq.54
  457.5 1.0 eq.55
  458.5 1.3 and.30
  459.8 1.5 and.31
  461.3 0.7 select_reduce_fusion
  462.0 0.7 broadcast_in_dim.81
  462.7 1.6 broadcast_in_dim.82
  464.4 0.6 eq.56
  465.0 1.4 eq.57
  466.4 1.7 reduce-precision_convert_fusion
  468.1 1.3 copy.93
  469.4 41.9 %all-to-all-done.3 = bf16[8,144,1024]{2,1,0:T(8,128)(2,1)S(1)} async-done(((bf16[8,144,1024]{2,1,0:T(8,128)(2,1)}), bf16[8,144,1024]{2,1,0:T(8,128)(2,1)S(1)}, u32[]{:S(2)}, u32[]{:S(2)}) %all-to-all-start.3) | async-done | bytes 2359328 | tf_op jit(solution)/shard_map/all_to_all | solution.py:180
  511.4 1.8 copy.92
  513.2 1.0 copy.102
  514.2 1.3 fusion.20
  515.5 1.2 fusion.17
  (56 shorter events, 1.7 us)
Async XLA Ops:
  7.2 3.0 copy-start.9
  7.2 70.2 %all-gather.2.cloned.1.call-start = ((), (), s32[]{:S(2)}) async-start(), calls=%async_computation.4 | async-start | bytes 2228224 | tf_op jit(solution)/shard_map/all_gather | solution.py:218
  10.3 67.1 %copy-start.7 = (pred[128,2,16]{0,2,1:T(8,128)(4,1)}, pred[128,2,16]{0,2,1:T(8,128)(4,1)S(1)}, u32[]{:S(2)}) copy-start(pred[128,2,16]{0,2,1:T(8,128)(4,1)S(1)} %copy.82) | copy-start | bytes 12292
  83.5 2.2 copy-start.3
  89.1 1.3 copy-start.4
  92.6 0.7 copy-start.8
  93.1 1.0 copy-start.1
  101.8 77.9 %all-to-all-start = ((bf16[8,144,1024]{2,1,0:T(8,128)(2,1)}), bf16[8,144,1024]{2,1,0:T(8,128)(2,1)S(1)}, u32[]{:S(2)}, u32[]{:S(2)}) async-start(bf16[8,144,1024]{2,1,0:T(8,128)(2,1)} %bitcast.95), calls=%async_computation | async-start | bytes 4718592 | tf_op jit(solution)/shard_map/all_to_all | solution.py:180
  134.3 125.9 %collective-permute-start = (bf16[512,3072]{1,0:T(8,128)(2,1)}, bf16[512,3072]{1,0:T(8,128)(2,1)}, u32[]{:S(2)}, u32[]{:S(2)}) collective-permute-start(bf16[512,3072]{1,0:T(8,128)(2,1)} %bitcast.56.in_own), channel_id=1, source_target_pairs={{0,16},{16,0},{32,48},{48,32},{64,80},{80,64},{96,112},{112,96},{1... | collective-permute-start | bytes 9437192 | tf_op jit(solution)/shard_map/ppermute | solution.py:175
  185.0 14.9 %copy-start = (bf16[1,1536,512]{2,1,0:T(8,128)(2,1)S(1)}, bf16[1,1536,512]{2,1,0:T(8,128)(2,1)}, u32[]{:S(2)}) copy-start(bf16[1,1536,512]{2,1,0:T(8,128)(2,1)} %param.17) | copy-start | bytes 4718596
  185.0 75.2 %all-to-all-start.1 = ((bf16[16,72,1024]{2,1,0:T(8,128)(2,1)}), bf16[16,72,1024]{2,1,0:T(8,128)(2,1)}, u32[]{:S(2)}, u32[]{:S(2)}) async-start(bf16[16,72,1024]{2,1,0:T(8,128)(2,1)} %copy.88), calls=%async_computation.1 | async-start | bytes 4718592 | tf_op jit(solution)/shard_map/all_to_all | solution.py:184
  199.9 60.3 %collective-permute-start.1 = (bf16[1536,512]{1,0:T(8,128)(2,1)S(1)}, bf16[1536,512]{1,0:T(8,128)(2,1)S(1)}, u32[]{:S(2)}, u32[]{:S(2)}) collective-permute-start(bf16[1536,512]{1,0:T(8,128)(2,1)S(1)} %bitcast.89), channel_id=1, source_target_pairs={{0,16},{16,0},{32,48},{48,32},{64,80},{80,64},{96,112},{112,96},{1... | collective-permute-start | bytes 4718600 | tf_op jit(solution)/shard_map/ppermute | solution.py:175
  452.8 15.3 %copy-start.2 = (bf16[2,16,128,128]{2,3,1,0:T(8,128)(2,1)S(1)}, bf16[2,16,128,128]{2,3,1,0:T(8,128)(2,1)}, u32[]{:S(2)}) copy-start(bf16[2,16,128,128]{2,3,1,0:T(8,128)(2,1)} %copy-done.1) | copy-start | bytes 3145732
  452.8 58.6 %all-to-all-start.3 = ((bf16[8,144,1024]{2,1,0:T(8,128)(2,1)}), bf16[8,144,1024]{2,1,0:T(8,128)(2,1)S(1)}, u32[]{:S(2)}, u32[]{:S(2)}) async-start(bf16[8,144,1024]{2,1,0:T(8,128)(2,1)} %copy.91), calls=%async_computation.3 | async-start | bytes 4718592 | tf_op jit(solution)/shard_map/all_to_all | solution.py:180
  513.2 1.0 copy-start.5
  513.2 1.0 copy-start.6
Sparse Core Ops, SparseCore 0:
  9.8 67.5 all-gather.1

commit v2 on v1

--- a/solution.py
+++ b/solution.py
@@ -31,7 +31,7 @@
 STRIPE = D // GROUP
 
 
-def expert_kernel(x_ref, in_own, in_oth, out_own, out_oth, y_ref, part, recv, hid, s_send, s_recv, h_send, h_recv):
+def expert_kernel(x_ref, in_own, in_one, in_two, out_own, y_ref, part, recv, hid, out_oth, s_send, s_recv, h_send, h_recv, w_sems):
     c = lax.axis_index("ctx")
     side = c % 2
     place = (c // 2) % 4
@@ -46,10 +46,17 @@
     def _():
         pl.semaphore_signal(barrier, inc=1, device_id={"ctx": c + 2}, device_id_type=pl.DeviceIdType.MESH)
 
-    pl.semaphore_wait(barrier, jnp.where((place > 0) & (place < 3), 2, 1))
+    pl.semaphore_signal(barrier, inc=1, device_id={"ctx": c + 1 - 2 * side}, device_id_type=pl.DeviceIdType.MESH)
+    pl.semaphore_wait(barrier, jnp.where((place > 0) & (place < 3), 3, 2))
+    weights = pltpu.make_async_remote_copy(
+        src_ref=out_own, dst_ref=out_oth, send_sem=w_sems.at[0], recv_sem=w_sems.at[1],
+        device_id={"ctx": c + 1 - 2 * side}, device_id_type=pl.DeviceIdType.MESH)
+    weights.start()
 
     own = pl.ds(pl.multiple_of(side * STRIPE, STRIPE), STRIPE)
     oth = pl.ds(pl.multiple_of((1 - side) * STRIPE, STRIPE), STRIPE)
+    one = pl.ds(pl.multiple_of((1 - side) * STRIPE, STRIPE), STRIPE // 2)
+    two = pl.ds(pl.multiple_of((1 - side) * STRIPE + STRIPE // 2, STRIPE // 2), STRIPE // 2)
 
     def sum_copy(d, i):
         target = jnp.where(d == 1, c + 2, c - 2)
@@ -67,7 +74,8 @@
         def tile(n, _):
             cols = pl.ds(pl.multiple_of(n * TILE, TILE), TILE)
             acc = jnp.dot(x_ref[d, b, :, own], in_own[:, cols], preferred_element_type=jnp.float32)
-            acc += jnp.dot(x_ref[d, b, :, oth], in_oth[:, cols], preferred_element_type=jnp.float32)
+            acc += jnp.dot(x_ref[d, b, :, one], in_one[:, cols], preferred_element_type=jnp.float32)
+            acc += jnp.dot(x_ref[d, b, :, two], in_two[:, cols], preferred_element_type=jnp.float32)
             part[d, pl.ds(b * PACK, PACK), :, cols] = acc.astype(jnp.bfloat16).reshape(PACK, CHUNK, TILE)
             return 0
         lax.fori_loop(0, 2 * FF // TILE, tile, 0)
@@ -85,6 +93,10 @@
                 return 0
             lax.fori_loop(0, 2, both, 0)
 
+        @pl.when(t == 3 * LAG + PACK - 1)
+        def _():
+            weights.wait_recv()
+
         def direction(d, _):
             pos = jnp.where(d == 1, place, 3 - place)
             i = t - LAG * pos
@@ -147,9 +159,10 @@
         return 0
 
     lax.fori_loop(0, COUNT, drain, 0)
-
-
-def experts(rows, in_own, in_oth, out_own, out_oth):
+    weights.wait_send()
+
+
+def experts(rows, in_own, in_one, in_two, out_own):
     vmem = pl.BlockSpec(memory_space=pltpu.VMEM)
     return pl.pallas_call(
         expert_kernel,
@@ -160,28 +173,92 @@
             pltpu.VMEM((2, COUNT, CHUNK, 2 * FF), jnp.bfloat16),
             pltpu.VMEM((2, COUNT, CHUNK, 2 * FF), jnp.bfloat16),
             pltpu.VMEM((2, COUNT, CHUNK, FF), jnp.bfloat16),
+            pltpu.VMEM((FF, STRIPE), jnp.bfloat16),
             pltpu.SemaphoreType.DMA((2, COUNT)),
             pltpu.SemaphoreType.DMA((2, COUNT)),
             pltpu.SemaphoreType.DMA((2, COUNT)),
             pltpu.SemaphoreType.DMA((2, COUNT)),
+            pltpu.SemaphoreType.DMA((2,)),
         ],
         compiler_params=pltpu.CompilerParams(collective_id=3, has_side_effects=True, vmem_limit_bytes=48 * 2**20),
         cost_estimate=pl.CostEstimate(flops=2 * ROWS * (PART * 2 * FF + FF * PART), bytes_accessed=14 * 2**20, transcendentals=HALF * FF),
         name="experts",
-    )(rows.reshape(2, COUNT // PACK, BLOCK, PART), in_own, in_oth, out_own, out_oth).reshape(ROWS, PART)
-
-
-def paired(array):
-    return lax.ppermute(array, "ctx", [(i, i ^ 1) for i in range(16)])
-
-
-def along_z(array):
-    groups = [[2 * z + side for z in range(N_Z)] for side in range(2)]
-    return lax.all_to_all(array, "ctx", split_axis=0, concat_axis=0, axis_index_groups=groups, tiled=True)
-
-
-def along_exp(array):
-    return lax.all_to_all(array, "exp", split_axis=0, concat_axis=0, tiled=True)
+    )(rows.reshape(2, COUNT // PACK, BLOCK, PART), in_own, in_one, in_two, out_own).reshape(ROWS, PART)
+
+
+def exchange_kernel(*refs):
+    if len(refs) == 7:
+        give_ref, half_ref, take_ref, got_ref, sends, recvs, keep = refs
+    else:
+        give_ref, take_ref, sends, recvs, keep = refs
+    c = lax.axis_index("ctx")
+    e = lax.axis_index("exp")
+    side, z = c % 2, c // 2
+    core, x, y = e % 2, (e // 2) % 4, e // 8
+    me = e * N_Z + z
+    total = N_EXP * N_Z
+
+    def partner(o):
+        s, g = o % N_Z, o // N_Z
+        dz = jnp.where(s % 2 == 1, (s + 1) // 2, (N_Z - s // 2) % N_Z)
+        there = (y + g // 8) % 2 * 8 + (x + (g // 2) % 4) % 4 * 2 + (core + g % 2) % 2
+        return there, (z + dz) % N_Z
+
+    def other_half():
+        return pltpu.make_async_remote_copy(
+            src_ref=half_ref, dst_ref=got_ref, send_sem=sends.at[1], recv_sem=recvs.at[1],
+            device_id={"ctx": c + 1 - 2 * side}, device_id_type=pl.DeviceIdType.MESH)
+
+    barrier = pltpu.get_barrier_semaphore()
+
+    def greet(o, _):
+        pe, pz = partner(o)
+        pl.semaphore_signal(barrier, inc=1, device_id={"exp": pe, "ctx": 2 * pz + side}, device_id_type=pl.DeviceIdType.MESH)
+        return 0
+
+    lax.fori_loop(1, total, greet, 0)
+    if len(refs) == 7:
+        pl.semaphore_signal(barrier, inc=1, device_id={"ctx": c + 1 - 2 * side}, device_id_type=pl.DeviceIdType.MESH)
+        pl.semaphore_wait(barrier, total)
+        other_half().start()
+    else:
+        pl.semaphore_wait(barrier, total - 1)
+
+    def send(o, _):
+        pe, pz = partner(o)
+        pltpu.make_async_remote_copy(
+            src_ref=give_ref.at[pe * N_Z + pz], dst_ref=take_ref.at[me], send_sem=sends.at[0], recv_sem=recvs.at[0],
+            device_id={"exp": pe, "ctx": 2 * pz + side}, device_id_type=pl.DeviceIdType.MESH).start()
+        return 0
+
+    lax.fori_loop(1, total, send, 0)
+    stay = pltpu.make_async_copy(give_ref.at[me], take_ref.at[me], keep)
+    stay.start()
+    stay.wait()
+    rest = pltpu.make_async_remote_copy(
+        src_ref=give_ref.at[pl.ds(0, total - 1)], dst_ref=take_ref.at[pl.ds(0, total - 1)], send_sem=sends.at[0],
+        recv_sem=recvs.at[0], device_id={"ctx": c + 1 - 2 * side}, device_id_type=pl.DeviceIdType.MESH)
+    rest.wait_recv()
+    rest.wait_send()
+    if len(refs) == 7:
+        other_half().wait()
+
+
+def exchanged(blocks, half=None):
+    vmem = pl.BlockSpec(memory_space=pltpu.VMEM)
+    given = [blocks] if half is None else [blocks, half]
+    shapes = [jax.ShapeDtypeStruct(g.shape, g.dtype) for g in given]
+    got = pl.pallas_call(
+        exchange_kernel,
+        out_shape=shapes,
+        in_specs=[vmem] * len(given),
+        out_specs=[vmem] * len(given),
+        scratch_shapes=[pltpu.SemaphoreType.DMA((2,)), pltpu.SemaphoreType.DMA((2,)), pltpu.SemaphoreType.DMA],
+        compiler_params=pltpu.CompilerParams(collective_id=4 + len(given), has_side_effects=True, vmem_limit_bytes=24 * 2**20),
+        cost_estimate=pl.CostEstimate(flops=0, bytes_accessed=16 * 2**20, transcendentals=0),
+        name="dispatch" if half is not None else "giveback",
+    )(*given)
+    return got
 
 
 def attention(queries, keys_values):
@@ -243,8 +320,7 @@
     tok = queries.shape[1]
     in_own = expert_in[0].reshape(STRIPE, 2 * FF)
     out_own = expert_out[0]
-    in_oth = paired(in_own)
-    out_oth = paired(out_own)
+    in_one = lax.ppermute(in_own[: STRIPE // 2], "ctx", [(i, i ^ 1) for i in range(16)])
 
     same = routing[0][:, :, None] == jnp.arange(EXPERTS)[None, None, :]
     gates = jnp.sum(jnp.where(same, gate_weights[0][:, :, None], 0.0), axis=1)
@@ -252,8 +328,7 @@
     earlier = jnp.arange(tok)[:, None] > jnp.arange(tok)[None, :]
     slot = jnp.dot(earlier.astype(jnp.bfloat16), hit.astype(jnp.bfloat16), preferred_element_type=jnp.float32)
     chosen = hit[:, :, None] & (slot[:, :, None] == jnp.arange(CAP, dtype=jnp.float32)[None, None, :])
-    chosen = chosen.reshape(tok, N_EXP, 2, CAP).transpose(0, 2, 1, 3)
-    spread = jnp.where(chosen, gates.reshape(tok, N_EXP, 2, 1).transpose(0, 2, 1, 3), 0.0).reshape(tok, EXPERTS * CAP)
+    spread = jnp.where(chosen, gates[:, :, None], 0.0).reshape(tok, EXPERTS * CAP)
     pick = chosen.reshape(tok, EXPERTS * CAP).astype(jnp.bfloat16)
     high = lax.reduce_precision(spread, 8, 7)
     low = spread - high
@@ -266,17 +341,13 @@
     ).astype(jnp.bfloat16)
 
     outgoing = lax.dot_general(pick, normed, (((0,), (0,)), ((), ())), preferred_element_type=jnp.float32)
-    outgoing = outgoing.astype(jnp.bfloat16).reshape(2, N_EXP * CAP, 4, PART).transpose(0, 2, 1, 3)
-    middle = along_z(outgoing.reshape(N_Z, N_EXP * CAP, PART))
-    middle = middle.reshape(N_Z, N_EXP, CAP, PART).transpose(1, 0, 2, 3)
-    rows = along_exp(middle.reshape(N_EXP, N_Z * CAP, PART)).reshape(ROWS, PART)
-
-    made = experts(rows, in_own, in_oth, out_own, out_oth)
-
-    middle = along_exp(made.reshape(N_EXP, N_Z * CAP, PART))
-    middle = middle.reshape(N_EXP, N_Z, CAP, PART).transpose(1, 0, 2, 3)
-    back = along_z(middle.reshape(N_Z, N_EXP * CAP, PART))
-    back = back.reshape(2, 4, N_EXP * CAP, PART).transpose(0, 2, 1, 3).reshape(EXPERTS * CAP, D)
+    outgoing = outgoing.astype(jnp.bfloat16).reshape(N_EXP, 2, CAP, 4, 8, 128).transpose(0, 1, 3, 2, 4, 5)
+    rows, in_two = exchanged(outgoing.reshape(N_EXP * N_Z, CAP, 8, 128), in_own[STRIPE // 2 :])
+
+    made = experts(rows.reshape(ROWS, PART), in_own, in_one, in_two, out_own)
+
+    (back,) = exchanged(made.reshape(N_EXP * N_Z, CAP, 8, 128))
+    back = back.reshape(N_EXP, 2, 4, CAP, 8, 128).transpose(0, 1, 3, 2, 4, 5).reshape(EXPERTS * CAP, D)
     mixed = jnp.dot(spread, back, preferred_element_type=jnp.float32)
     mixed = mixed[:tok] + mixed[tok:]
     return (attended[None], mixed.astype(jnp.bfloat16)[None])

time: 525 us -> 462 us (0.88)
  Pallas kernels: 137 us -> 318 us
  waiting for transfers between devices: 214 us -> 62.8 us
  blocking collectives: 50.4 us -> 0 us
  starting transfers between devices: 48 us -> 2.16 us
    pallas_call x0 -> x2, Pallas kernels: none -> 175 us  [exchanged(): pl.pallas_call(exchange_kernel, out_shape=shapes, in_specs=[vmem] * len(g...]
    all_to_all x3 -> x0, waiting for transfers between devices: 86.5 us -> none  [the longest x2 86.5 us: along_z(): lax.all_to_all(array, 'ctx', split_axis=0, concat_axis=0, axis_index_grou...]
    ppermute x2 -> x1, waiting for transfers between devices: 60.2 us -> 0.01 us  [local(): lax.ppermute(in_own[:STRIPE // 2], 'ctx', [(i, i ^ 1) for i in range(16)])]
    all_to_all x1 -> x0, blocking collectives: 50.4 us -> none  [along_exp(): return lax.all_to_all(array, 'exp', split_axis=0, concat_axis=0, tiled=True)]
    all_to_all x3 -> x0, starting transfers between devices: 47.1 us -> none  [the longest x2 32.2 us: along_z(): lax.all_to_all(array, 'ctx', split_axis=0, concat_axis=0, axis_index_grou...]
    unnamed x22 -> x31, local copies, waits for them, and re-layouts: 11.9 us -> 22.5 us
    reshape x5 -> x3, local copies, waits for them, and re-layouts: 14.1 us -> 6 us  [the longest x2 5.59 us: local(): back.reshape(N_EXP, 2, 4, CAP, 8, 128).transpose(0, 1, 3, 2, 4, 5)]
    pallas_call x1, Pallas kernels: 137 us -> 143 us  [experts(): pl.pallas_call(expert_kernel, out_shape=jax.ShapeDtypeStruct((2, COUNT //...]
  transfers between devices with their start and end apart: 6 -> 2, of which waited for: 4 -> 1; matrix products, arithmetic and copies ran while one was open for 5% -> 10% of each run, Pallas kernels for 0% -> 23%
where the time goes in v2:
time: 462 us
  Pallas kernels  318 us (69%)
  waiting for transfers between devices  62.8 us (14%)
  local copies, waits for them, and re-layouts  48.5 us (10%)
  between operations  14.2 us (3%)
  other arithmetic  8.23 us (2%)
  matrix products  7.03 us (2%)
    pallas_call x2, Pallas kernels, exchanged(): pl.pallas_call(exchange_kernel, out_shape=shapes, in_specs=[vmem] * len(g...  175 us
    pallas_call x1, Pallas kernels, experts(): pl.pallas_call(expert_kernel, out_shape=jax.ShapeDtypeStruct((2, COUNT //...  143 us
    all_gather x1, waiting for transfers between devices, attention(): piece = lax.all_gather(keys_values, 'ctx', axis=1, tiled=True)  62.1 us
    unnamed x31, local copies, waits for them, and re-layouts  22.5 us
  transfers between devices with their start and end apart: 2, of which 1 were waited for; matrix products, arithmetic and copies ran while one was open for 10% of the time, Pallas kernels for 23%

profile of v2, /device:TPU:1, one launch (start us, length us, event | category | flops | bytes accessed | tf_op | source)
XLA Modules:
  0.0 461.7 jit_solution(3023811694492485383)
XLA Ops:
  7.2 0.7 all-gather.2.cloned.1.call-update
  7.9 4.9 %fusion.29 = (bf16[1,256,2,1536]{3,2,1,0:T(2,128)(2,1)S(1)}, bf16[1,256,2,1536]{3,2,1,0:T(2,128)(2,1)}) fusion(bf16[1,512,2,1536]{3,2,1,0:T(2,128)(2,1)} %param.16), kind=kLoop, calls=%fused_computation.48 | loop fusion | bytes 6291456 | tf_op jit(solution)/shard_map/slice | solution.py:323
  12.8 1.5 copy.58
  14.3 2.1 collective-permute-start
  16.4 1.6 copy.41
  18.0 1.3 copy.43
  19.4 0.1 fusion.26
  19.6 0.7 and.28
  20.2 1.8 copy.56
  22.0 0.6 copy-done.5
  22.6 2.4 copy.57
  25.0 0.7 and.24
  25.7 0.6 and.25
  26.4 0.7 select_reduce_fusion
  27.2 0.7 broadcast_in_dim.80
  27.9 1.0 reduce-precision_convert_fusion
  29.0 62.1 %all-gather.2.cloned.1.call-done = bf16[1,2048,512]{2,1,0:T(8,128)(2,1)} async-done(((bf16[1,128,512]{2,1,0:T(8,128)(2,1)}), bf16[1,2048,512]{2,1,0:T(8,128)(2,1)}) %all-gather.2.cloned.1.call-update) | async-done | bytes 2097168 | tf_op jit(solution)/shard_map/all_gather | solution.py:295
  91.1 4.1 copy.42
  95.3 1.6 broadcast_in_dim.75
  96.9 10.0 %while.20 = (s32[]{:T(128)}, f32[2,16,128]{2,1,0:T(8,128)S(1)}, f32[2,16,128]{2,1,0:T(8,128)S(1)}, f32[2,16,128,128]{3,2,1,0:T(8,128)}, s32[]{:T(128)}, /*index=...) while((s32[]{:T(128)}, f32[2,16,128]{2,1,0:T(8,128)S(1)}, ...), condition=%wide.region_5.6_spmd.clone, body=%wide.region_0.5_spmd.clone.sunk | while | flops 1102127744 | bytes 54532472 | solution.py:310
  96.9 9.8 %conditional.3 = (f32[2,16,128]{2,1,0:T(8,128)S(1)}, f32[2,16,128]{2,1,0:T(8,128)S(1)}, f32[2,16,128,128]{3,2,1,0:T(8,128)}) conditional(s32[]{:T(128)} %convert_element_type.87, (s32[]{:T(128)}, s32[]{:T(128)}, s32[]{:T(128)}, bf16[4,512,512]{1,2,0:T(8,128)(2,1)}, bf16[128,2,16,128]{3,0,2,1:T(8,128)(2,1)}, /*index=5*/f32[2,16,128]{2,1,0:T(8,128)S(1)}, ...), branch_computations={%region_1.0_spmd, %region_4.4_spmd} | conditional | flops 1102127744 | bytes 54498972 | solution.py:303
  96.9 1.2 dynamic-slice_bitcast_fusion
  98.2 0.1 broadcast_compare_fusion
  98.3 1.4 fusion.2
  99.8 2.1 fusion.4
  102.0 3.4 multiply_add_fusion
  105.4 1.4 copy-done.9
  107.0 2.9 copy.44
  109.9 2.2 fusion.13
  112.1 1.0 copy-done.6
  113.1 0.7 fusion.15
  113.8 0.8 fusion.17
  114.6 0.5 copy.55
  115.1 0.4 copy.45
  115.5 104.7 %dispatch.1 = (bf16[128,9,8,128]{3,2,1,0:T(8,128)(2,1)S(1)}, bf16[256,3072]{1,0:T(8,128)(2,1)S(1)}) custom-call(bf16[128,9,8,128]{3,2,1,0:T(8,128)(2,1)S(1)} %bitcast.83, bf16[256,3072]{1,0:T(8,128)(2,1)S(1)} %bitcast.86), custom_call_target="tpu_custom_call" | custom-call | bytes 16777216 | tf_op jit(solution)/shard_map/dispatch/pallas_call | solution.py:251
  220.2 1.4 copy-done
  221.6 1.1 copy-done.2
  222.8 5.1 %reshape_reshape.6.x_ref = bf16[2,6,96,1024]{3,2,1,0:T(8,128)(2,1)} reshape(bf16[128,9,8,128]{3,2,1,0:T(8,128)(2,1)} %copy-done) | data formatting | bytes 4718592 | tf_op jit(solution)/shard_map/reshape;reshape | solution.py:186
  227.9 1.4 copy-done.3
  229.3 143.1 %experts.1 = bf16[2,6,96,1024]{3,2,1,0:T(8,128)(2,1)} custom-call(bf16[2,6,96,1024]{3,2,1,0:T(8,128)(2,1)} %reshape_reshape.6.x_ref, bf16[512,3072]{1,0:T(8,128)(2,1)} %bitcast.98, bf16[256,3072]{1,0:T(8,128)(2,1)S(1)} %collective-permute-done.in_one, bf16[256,3072]{1,0:T(8,128)(2,1)S(1)} %copy-done.3, bf16[1536,512]{1,0:T(8,128)(2,1)S(1)} %bitcast.87), custom_call_target="tpu_custom_call" | custom-call | flops 10871635968 | bytes 14680064 | tf_op jit(solution)/shard_map/experts/pallas_call | solution.py:167
  372.4 2.3 copy.59
  374.7 70.5 %giveback.1 = bf16[128,9,8,128]{3,2,1,0:T(8,128)(2,1)S(1)} custom-call(bf16[128,9,8,128]{3,2,1,0:T(8,128)(2,1)S(1)} %bitcast.84), custom_call_target="tpu_custom_call" | custom-call | bytes 16777216 | tf_op jit(solution)/shard_map/giveback/pallas_call | solution.py:251
  445.2 2.0 copy.61
  447.2 3.6 reshape.118
  450.8 1.3 fusion.21
  452.1 1.2 fusion.18
  453.3 0.2 copy-done.7
  453.5 1.3 copy.47
  (52 shorter events, 0.5 us)
Async XLA Ops:
  7.2 84.0 %all-gather.2.cloned.1.call-start = ((), (), s32[]{:S(2)}) async-start(), calls=%async_computation | async-start | bytes 2228224 | tf_op jit(solution)/shard_map/all_gather | solution.py:295
  14.3 5.1 %copy-start.13 = (s32[1,128,8]{1,2,0:T(8,128)S(1)}, s32[1,128,8]{1,2,0:T(8,128)}, u32[]{:S(2)}) copy-start(s32[1,128,8]{1,2,0:T(8,128)} %param.14) | copy-start | bytes 12292
  14.3 213.6 %collective-permute-start = (bf16[256,3072]{1,0:T(8,128)(2,1)}, bf16[256,3072]{1,0:T(8,128)(2,1)S(1)}, u32[]{:S(2)}, u32[]{:S(2)}) collective-permute-start(bf16[256,3072]{1,0:T(8,128)(2,1)} %bitcast.46), channel_id=1, source_target_pairs={{0,16},{16,0},{32,48},{48,32},{64,80},{80,64},{96,112},{112,96},{1... | collective-permute-start | bytes 4718600 | tf_op jit(solution)/shard_map/ppermute | solution.py:323
  19.3 0.9 copy-start.11
  20.2 2.4 copy-start.5
  96.9 1.4 copy-start.4
  99.8 2.2 copy-start.8
  105.4 1.4 copy-start.9
  109.9 3.2 copy-start.12
  109.9 3.9 copy-start.10
  112.1 1.0 copy-start.6
  220.2 1.4 copy-start
  221.6 1.1 copy-start.2
  222.8 5.1 %copy-start.1 = (bf16[1,1536,512]{2,1,0:T(8,128)(2,1)S(1)}, bf16[1,1536,512]{2,1,0:T(8,128)(2,1)}, u32[]{:S(2)}) copy-start(bf16[1,1536,512]{2,1,0:T(8,128)(2,1)} %param.17) | copy-start | bytes 4718596
  227.9 1.4 copy-start.3
  452.1 1.4 copy-start.7
Sparse Core Ops, SparseCore 0:
  9.8 81.3 all-gather.1

commit v3 on v2

--- a/solution.py
+++ b/solution.py
@@ -17,21 +17,24 @@
 GROUP = 8
 CAP = 9
 EXPERTS = 32
+TOK = 128
+SLOTS = EXPERTS * CAP
 N_EXP = 16
 N_Z = 8
 ROWS = N_EXP * N_Z * CAP
 HALF = ROWS // 2
-CHUNK = 32
+CHUNK = 16
 COUNT = HALF // CHUNK
-PACK = 3
+PACK = 9
 BLOCK = CHUNK * PACK
 LAG = 2
 TILE = 512
 PART = D // 4
 STRIPE = D // GROUP
-
-
-def expert_kernel(x_ref, in_own, in_one, in_two, out_own, y_ref, part, recv, hid, out_oth, s_send, s_recv, h_send, h_recv, w_sems):
+GATHER = BLOCK // CAP
+
+
+def expert_kernel(x_ref, in_own, in_one, in_two, out_own, y_ref, part, recv, hid, out_oth, flat, xb, s_send, s_recv, h_send, h_recv, w_sems):
     c = lax.axis_index("ctx")
     side = c % 2
     place = (c // 2) % 4
@@ -71,19 +74,28 @@
             device_id={"ctx": target}, device_id_type=pl.DeviceIdType.MESH)
 
     def products(d, b):
+        flat[...] = x_ref[d, b].astype(jnp.float32).reshape(8 * BLOCK, 128)
+        for k in range(8):
+            xb[:, k * 128 : (k + 1) * 128] = flat[pl.ds(k, BLOCK, stride=8), :].astype(jnp.bfloat16)
+
         def tile(n, _):
             cols = pl.ds(pl.multiple_of(n * TILE, TILE), TILE)
-            acc = jnp.dot(x_ref[d, b, :, own], in_own[:, cols], preferred_element_type=jnp.float32)
-            acc += jnp.dot(x_ref[d, b, :, one], in_one[:, cols], preferred_element_type=jnp.float32)
-            acc += jnp.dot(x_ref[d, b, :, two], in_two[:, cols], preferred_element_type=jnp.float32)
+            acc = jnp.dot(xb[:, own], in_own[:, cols], preferred_element_type=jnp.float32)
+            acc += jnp.dot(xb[:, one], in_one[:, cols], preferred_element_type=jnp.float32)
+            acc += jnp.dot(xb[:, two], in_two[:, cols], preferred_element_type=jnp.float32)
             part[d, pl.ds(b * PACK, PACK), :, cols] = acc.astype(jnp.bfloat16).reshape(PACK, CHUNK, TILE)
             return 0
         lax.fori_loop(0, 2 * FF // TILE, tile, 0)
 
     def result(d, b):
         rows = hid[d, pl.ds(b * PACK, PACK)].reshape(BLOCK, FF)
-        y_ref[d, b, :, own] = jnp.dot(rows, out_own[...], preferred_element_type=jnp.float32).astype(jnp.bfloat16)
-        y_ref[d, b, :, oth] = jnp.dot(rows, out_oth[...], preferred_element_type=jnp.float32).astype(jnp.bfloat16)
+        mine = jnp.dot(rows, out_own[...], preferred_element_type=jnp.float32)
+        theirs = jnp.dot(rows, out_oth[...], preferred_element_type=jnp.float32)
+        for k in range(4):
+            cols = slice(k * 128, (k + 1) * 128)
+            flat[pl.ds(k, BLOCK, stride=8), :] = jnp.where(side == 0, mine[:, cols], theirs[:, cols])
+            flat[pl.ds(k + 4, BLOCK, stride=8), :] = jnp.where(side == 0, theirs[:, cols], mine[:, cols])
+        y_ref[d, b] = flat[...].astype(jnp.bfloat16).reshape(GATHER, CAP, 8, 128)
 
     def step(t, _):
         @pl.when((t % PACK == 0) & (t < COUNT))
@@ -166,7 +178,7 @@
     vmem = pl.BlockSpec(memory_space=pltpu.VMEM)
     return pl.pallas_call(
         expert_kernel,
-        out_shape=jax.ShapeDtypeStruct((2, COUNT // PACK, BLOCK, PART), jnp.bfloat16),
+        out_shape=jax.ShapeDtypeStruct((2, COUNT // PACK, GATHER, CAP, 8, 128), jnp.bfloat16),
         in_specs=[vmem] * 5,
         out_specs=vmem,
         scratch_shapes=[
@@ -174,6 +186,8 @@
             pltpu.VMEM((2, COUNT, CHUNK, 2 * FF), jnp.bfloat16),
             pltpu.VMEM((2, COUNT, CHUNK, FF), jnp.bfloat16),
             pltpu.VMEM((FF, STRIPE), jnp.bfloat16),
+            pltpu.VMEM((8 * BLOCK, 128), jnp.float32),
+            pltpu.VMEM((BLOCK, PART), jnp.bfloat16),
             pltpu.SemaphoreType.DMA((2, COUNT)),
             pltpu.SemaphoreType.DMA((2, COUNT)),
             pltpu.SemaphoreType.DMA((2, COUNT)),
@@ -183,7 +197,7 @@
         compiler_params=pltpu.CompilerParams(collective_id=3, has_side_effects=True, vmem_limit_bytes=48 * 2**20),
         cost_estimate=pl.CostEstimate(flops=2 * ROWS * (PART * 2 * FF + FF * PART), bytes_accessed=14 * 2**20, transcendentals=HALF * FF),
         name="experts",
-    )(rows.reshape(2, COUNT // PACK, BLOCK, PART), in_own, in_one, in_two, out_own).reshape(ROWS, PART)
+    )(rows.reshape(2, COUNT // PACK, GATHER, CAP, 8, 128), in_own, in_one, in_two, out_own)
 
 
 def exchange_kernel(*refs):
@@ -261,96 +275,245 @@
     return got
 
 
-def attention(queries, keys_values):
-    tok = queries.shape[1]
-    share = QH // KVH
-    first = lax.axis_index("ctx") * tok
-    local_q = queries[0].reshape(tok, KVH, share, HEAD)
-    query_place = first + jnp.arange(tok)
-
-    def compute(state, block_rows, start):
-        running, total, accum = state
-        count = block_rows.shape[0]
-        keys = block_rows[:, : KVH * HEAD].reshape(count, KVH, HEAD)
-        vals = block_rows[:, KVH * HEAD :].reshape(count, KVH, HEAD)
-        scores = jnp.einsum(
-            "qkgh,nkh->kgqn", local_q, keys, preferred_element_type=jnp.float32
-        ) / math.sqrt(HEAD)
-        allowed = (start + jnp.arange(count))[None, :] <= query_place[:, None]
-        scores = jnp.where(allowed, scores, -1e30)
-        newest = jnp.maximum(running, jnp.max(scores, axis=-1))
-        keep = jnp.exp(running - newest)
-        weights = jnp.where(allowed, jnp.exp(scores - newest[..., None]), 0.0)
-        total = total * keep + jnp.sum(weights, axis=-1)
-        accum = accum * keep[..., None] + jnp.einsum(
-            "kgqn,nkh->kgqh", weights.astype(jnp.bfloat16), vals, preferred_element_type=jnp.float32
-        )
-        return (newest, total, accum)
-
-    initial = (
-        jnp.full((KVH, share, tok), -1e30, jnp.float32),
-        jnp.zeros((KVH, share, tok), jnp.float32),
-        jnp.zeros((KVH, share, tok, HEAD), jnp.float32),
-    )
-    piece = lax.all_gather(keys_values, "ctx", axis=1, tiled=True)
-    count = piece.shape[1]
-    block = tok * 4
-    blocks = piece[0].reshape(count // block, block, piece.shape[2])
-
-    def visit(index, kept):
-        block_rows = lax.dynamic_index_in_dim(blocks, index, 0, keepdims=False)
-        block_start = index * block
-        return lax.cond(
-            block_start > first + tok - 1,
-            lambda inner: inner,
-            lambda inner: compute(inner, block_rows, block_start),
-            kept,
-        )
-
-    running, total, accum = lax.fori_loop(0, count // block, visit, initial)
-    return (
-        (accum / total[..., None])
-        .transpose(2, 0, 1, 3)
-        .reshape(tok, QH * HEAD)
-        .astype(jnp.bfloat16)
-    )
+def attention_kernel(q_ref, kv_ref, gain_ref, routing_ref, gate_ref, half_ref, att_ref, rows_ref, spread_ref, got_ref,
+                     qs, kv, acc, top, normed, flat, near, sends, recvs, w_sems):
+    c = lax.axis_index("ctx")
+    side, z = c % 2, c // 2
+    mate = c + 1 - 2 * side
+
+    def to(target):
+        return dict(device_id={"ctx": target}, device_id_type=pl.DeviceIdType.MESH)
+
+    def ring(way, d, which, block):
+        target = jnp.where(way == 0, (z + 1) % N_Z, (z + N_Z - 1) % N_Z) * 2 + side
+        return pltpu.make_async_remote_copy(
+            src_ref=kv.at[block], dst_ref=kv.at[block], send_sem=sends.at[way, d, which], recv_sem=recvs.at[block], **to(target))
+
+    def arrived(block):
+        pltpu.make_async_remote_copy(
+            src_ref=kv.at[block], dst_ref=kv.at[block], send_sem=near.at[0], recv_sem=recvs.at[block], **to(mate)).wait_recv()
+
+    pair = pltpu.make_async_remote_copy(
+        src_ref=kv.at[c], dst_ref=kv.at[c], send_sem=near.at[0], recv_sem=recvs.at[c], **to(mate))
+    weights = pltpu.make_async_remote_copy(
+        src_ref=half_ref, dst_ref=got_ref, send_sem=w_sems.at[0], recv_sem=w_sems.at[1], **to(mate))
+
+    barrier = pltpu.get_barrier_semaphore()
+    for target in (mate, (z + 1) % N_Z * 2 + side, (z + N_Z - 1) % N_Z * 2 + side):
+        pl.semaphore_signal(barrier, inc=1, **to(target))
+    kv[c] = kv_ref[...]
+    pl.semaphore_wait(barrier, 3)
+    pair.start()
+    ring(0, 0, 0, c).start()
+    ring(1, 0, 0, c).start()
+
+    for h in range(QH):
+        qs[pl.ds(h * TOK, TOK), :] = q_ref[:, h * HEAD : (h + 1) * HEAD]
+
+    lanes = lax.broadcasted_iota(jnp.int32, (TOK, 128), 1)
+    hit = jnp.zeros((TOK, 128), jnp.float32)
+    gates = jnp.zeros((TOK, 128), jnp.float32)
+    for k in range(TOP):
+        same = (routing_ref[:, k : k + 1] == lanes) & (lanes < EXPERTS)
+        hit = jnp.where(same, 1.0, hit)
+        gates = jnp.where(same, gate_ref[:, k : k + 1], gates)
+    earlier = lax.broadcasted_iota(jnp.int32, (TOK, TOK), 0) > lax.broadcasted_iota(jnp.int32, (TOK, TOK), 1)
+    earlier = jnp.where(earlier, 1.0, 0.0).astype(jnp.bfloat16)
+    slot = jnp.dot(earlier, hit.astype(jnp.bfloat16), preferred_element_type=jnp.float32)
+    expert = lax.broadcasted_iota(jnp.int32, (128, SLOTS), 0)
+    column = lax.broadcasted_iota(jnp.int32, (128, SLOTS), 1)
+    begin = expert * CAP
+    widen = jnp.where((column >= begin) & (column < begin + CAP), 1.0, 0.0).astype(jnp.bfloat16)
+
+    def wide(part):
+        return jnp.dot(part.astype(jnp.bfloat16), widen, preferred_element_type=jnp.float32)
+
+    inside = jnp.where((column >= begin) & (column < begin + CAP), column - begin, 0).astype(jnp.float32)
+    number = jnp.sum(inside, axis=0, keepdims=True)
+    chosen = (wide(hit) > 0.5) & (wide(slot) == number)
+    high = gates.astype(jnp.bfloat16).astype(jnp.float32)
+    spread_ref[0:TOK, :] = jnp.where(chosen, wide(high), 0.0).astype(jnp.bfloat16)
+    spread_ref[TOK : 2 * TOK, :] = jnp.where(chosen, wide(gates - high), 0.0).astype(jnp.bfloat16)
+    pick = jnp.where(chosen, 1.0, 0.0).T.astype(jnp.bfloat16)
+
+    arrived(mate)
+    ring(0, 0, 1, mate).start()
+    ring(1, 0, 1, mate).start()
+    weights.start()
+
+    scale = math.log2(math.e) / math.sqrt(HEAD)
+    chunk = 2 * TOK
+
+    def attend(zk, diagonal):
+        for g in range(KVH):
+            keys = kv[pl.ds(2 * zk, 2), :, g * HEAD : (g + 1) * HEAD].reshape(2 * TOK, HEAD)
+            vals = kv[pl.ds(2 * zk, 2), :, (KVH + g) * HEAD : (KVH + g + 1) * HEAD].reshape(2 * TOK, HEAD)
+            vals = jnp.concatenate([vals, jnp.ones((2 * TOK, HEAD), jnp.bfloat16)], axis=1)
+
+            def rows(n, _):
+                here = pl.ds(pl.multiple_of(g * (QH // KVH) * TOK + n * chunk, chunk), chunk)
+                score = scale * lax.dot_general(qs[here, :], keys, (((1,), (1,)), ((), ())), preferred_element_type=jnp.float32)
+                if diagonal:
+                    token = lax.broadcasted_iota(jnp.int32, (chunk, 2 * TOK), 0) % TOK
+                    place = lax.broadcasted_iota(jnp.int32, (chunk, 2 * TOK), 1)
+                    score = jnp.where(place <= token + TOK * side, score, -1e30)
+                    newest = jnp.broadcast_to(jnp.max(score, axis=1, keepdims=True), (chunk, HEAD))
+                else:
+                    before = top[here, :]
+                    newest = jnp.maximum(before, jnp.max(score, axis=1, keepdims=True))
+                probs = jnp.exp2(score - jnp.concatenate([newest, newest], axis=1)).astype(jnp.bfloat16)
+                made = jnp.dot(probs, vals, preferred_element_type=jnp.float32)
+                if not diagonal:
+                    keep = jnp.exp2(before - newest)
+                    made += acc[here, :] * jnp.concatenate([keep, keep], axis=1)
+                acc[here, :] = made
+                top[here, :] = newest
+                return 0
+
+            lax.fori_loop(0, QH // KVH * TOK // chunk, rows, 0, unroll=2)
+
+    attend(z, True)
+
+    def stage(d, _):
+        low, up = (z + N_Z - d) % N_Z, (z + d) % N_Z
+
+        @pl.when(d < 4)
+        def _():
+            def one(w, _):
+                y = (side + w) % 2
+                arrived(2 * low + y)
+
+                @pl.when((d < 3) | (y == 0))
+                def _():
+                    ring(0, d, w, 2 * low + y).start()
+                arrived(2 * up + y)
+
+                @pl.when((d < 3) | (y == 1))
+                def _():
+                    ring(1, d, w, 2 * up + y).start()
+                return 0
+            lax.fori_loop(0, 2, one, 0)
+
+        @pl.when(d == 4)
+        def _():
+            arrived(2 * up)
+            arrived(2 * up + 1)
+
+        def way(w, _):
+            zk = jnp.where(w == 0, low, up)
+
+            @pl.when((zk < z) & ((d < 4) | (w == 0)))
+            def _():
+                attend(zk, False)
+            return 0
+        lax.fori_loop(0, 2, way, 0)
+        return 0
+
+    lax.fori_loop(1, 5, stage, 0)
+
+    squares = jnp.zeros((TOK, HEAD), jnp.float32)
+    for h in range(QH):
+        here = pl.ds(h * TOK, TOK)
+        out = (acc[here, 0:HEAD] / acc[here, HEAD : 2 * HEAD]).astype(jnp.bfloat16)
+        att_ref[:, h * HEAD : (h + 1) * HEAD] = out
+        out = out.astype(jnp.float32)
+        squares += out * out
+    root = lax.rsqrt(jnp.sum(squares, axis=1, keepdims=True) / D + 1e-06)
+    for h in range(QH):
+        cols = slice(h * HEAD, (h + 1) * HEAD)
+        normed[:, cols] = (att_ref[:, cols].astype(jnp.float32) * root * gain_ref[:, cols]).astype(jnp.bfloat16)
+    for n in range(4):
+        cols = slice(n * PART, (n + 1) * PART)
+        picked = jnp.dot(pick, normed[:, cols], preferred_element_type=jnp.float32)
+        for k in range(8):
+            flat[pl.ds(k, SLOTS, stride=8), :] = picked[:, k * 128 : (k + 1) * 128]
+        rows_ref[:, n] = flat[...].astype(jnp.bfloat16).reshape(EXPERTS, CAP, 8, 128)
+
+    pair.wait_send()
+
+    def drain(d, _):
+        def one(w, _):
+            y = (side + w) % 2
+
+            @pl.when((d < 3) | (y == 0))
+            def _():
+                ring(0, d, w, c).wait_send()
+
+            @pl.when((d < 3) | (y == 1))
+            def _():
+                ring(1, d, w, c).wait_send()
+            return 0
+        return lax.fori_loop(0, 2, one, 0)
+
+    lax.fori_loop(0, 4, drain, 0)
+    weights.wait()
+
+
+def attention(queries, keys_values, gain, routing, gate_weights, half):
+    vmem = pl.BlockSpec(memory_space=pltpu.VMEM)
+    return pl.pallas_call(
+        attention_kernel,
+        out_shape=[
+            jax.ShapeDtypeStruct((TOK, D), jnp.bfloat16),
+            jax.ShapeDtypeStruct((EXPERTS, 4, CAP, 8, 128), jnp.bfloat16),
+            jax.ShapeDtypeStruct((2 * TOK, SLOTS), jnp.bfloat16),
+            jax.ShapeDtypeStruct(half.shape, half.dtype),
+        ],
+        in_specs=[vmem] * 6,
+        out_specs=[vmem] * 4,
+        scratch_shapes=[
+            pltpu.VMEM((QH * TOK, HEAD), jnp.bfloat16),
+            pltpu.VMEM((2 * N_Z, TOK, 2 * KVH * HEAD), jnp.bfloat16),
+            pltpu.VMEM((QH * TOK, 2 * HEAD), jnp.float32),
+            pltpu.VMEM((QH * TOK, HEAD), jnp.float32),
+            pltpu.VMEM((TOK, D), jnp.bfloat16),
+            pltpu.VMEM((8 * SLOTS, 128), jnp.float32),
+            pltpu.SemaphoreType.DMA((1,)),
+            pltpu.SemaphoreType.DMA((2, 4, 2)),
+            pltpu.SemaphoreType.DMA((2 * N_Z,)),
+            pltpu.SemaphoreType.DMA((2,)),
+        ],
+        compiler_params=pltpu.CompilerParams(collective_id=1, has_side_effects=True, vmem_limit_bytes=40 * 2**20),
+        cost_estimate=pl.CostEstimate(flops=4 * TOK * 2048 * D, bytes_accessed=8 * 2**20, transcendentals=TOK * 2048 * QH),
+        name="attention",
+    )(queries, keys_values, gain, routing, gate_weights, half)
+
+
+def combine_kernel(back_ref, spread_ref, mixed_ref, flat, cols):
+    def quarter(n, _):
+        flat[...] = back_ref[:, n].astype(jnp.float32).reshape(8 * SLOTS, 128)
+        for k in range(8):
+            cols[:, k * 128 : (k + 1) * 128] = flat[pl.ds(k, SLOTS, stride=8), :].astype(jnp.bfloat16)
+        total = jnp.dot(spread_ref[...], cols[...], preferred_element_type=jnp.float32)
+        mixed_ref[:, pl.ds(pl.multiple_of(n * PART, PART), PART)] = (total[:TOK] + total[TOK:]).astype(jnp.bfloat16)
+        return 0
+    lax.fori_loop(0, 4, quarter, 0)
+
+
+def combine(back, spread):
+    vmem = pl.BlockSpec(memory_space=pltpu.VMEM)
+    return pl.pallas_call(
+        combine_kernel,
+        out_shape=jax.ShapeDtypeStruct((TOK, D), jnp.bfloat16),
+        in_specs=[vmem] * 2,
+        out_specs=vmem,
+        scratch_shapes=[pltpu.VMEM((8 * SLOTS, 128), jnp.float32), pltpu.VMEM((SLOTS, PART), jnp.bfloat16)],
+        compiler_params=pltpu.CompilerParams(vmem_limit_bytes=24 * 2**20),
+        name="combine",
+    )(back, spread)
 
 
 def local(queries, keys_values, norm_gain, routing, gate_weights, expert_in, expert_out):
-    tok = queries.shape[1]
     in_own = expert_in[0].reshape(STRIPE, 2 * FF)
     out_own = expert_out[0]
-    in_one = lax.ppermute(in_own[: STRIPE // 2], "ctx", [(i, i ^ 1) for i in range(16)])
-
-    same = routing[0][:, :, None] == jnp.arange(EXPERTS)[None, None, :]
-    gates = jnp.sum(jnp.where(same, gate_weights[0][:, :, None], 0.0), axis=1)
-    hit = jnp.any(same, axis=1)
-    earlier = jnp.arange(tok)[:, None] > jnp.arange(tok)[None, :]
-    slot = jnp.dot(earlier.astype(jnp.bfloat16), hit.astype(jnp.bfloat16), preferred_element_type=jnp.float32)
-    chosen = hit[:, :, None] & (slot[:, :, None] == jnp.arange(CAP, dtype=jnp.float32)[None, None, :])
-    spread = jnp.where(chosen, gates[:, :, None], 0.0).reshape(tok, EXPERTS * CAP)
-    pick = chosen.reshape(tok, EXPERTS * CAP).astype(jnp.bfloat16)
-    high = lax.reduce_precision(spread, 8, 7)
-    low = spread - high
-    spread = jnp.concatenate([high, low], axis=0).astype(jnp.bfloat16)
-
-    attended = attention(queries, keys_values)
-    values = attended.astype(jnp.float32)
-    normed = (
-        values * lax.rsqrt(jnp.mean(values * values, axis=-1, keepdims=True) + 1e-06) * norm_gain
-    ).astype(jnp.bfloat16)
-
-    outgoing = lax.dot_general(pick, normed, (((0,), (0,)), ((), ())), preferred_element_type=jnp.float32)
-    outgoing = outgoing.astype(jnp.bfloat16).reshape(N_EXP, 2, CAP, 4, 8, 128).transpose(0, 1, 3, 2, 4, 5)
-    rows, in_two = exchanged(outgoing.reshape(N_EXP * N_Z, CAP, 8, 128), in_own[STRIPE // 2 :])
-
-    made = experts(rows.reshape(ROWS, PART), in_own, in_one, in_two, out_own)
-
-    (back,) = exchanged(made.reshape(N_EXP * N_Z, CAP, 8, 128))
-    back = back.reshape(N_EXP, 2, 4, CAP, 8, 128).transpose(0, 1, 3, 2, 4, 5).reshape(EXPERTS * CAP, D)
-    mixed = jnp.dot(spread, back, preferred_element_type=jnp.float32)
-    mixed = mixed[:tok] + mixed[tok:]
-    return (attended[None], mixed.astype(jnp.bfloat16)[None])
+    attended, outgoing, spread, in_one = attention(
+        queries[0], keys_values[0], norm_gain[None], routing[0], gate_weights[0], in_own[: STRIPE // 2])
+    blocks = (N_EXP * N_Z, CAP, 8, 128)
+    rows, in_two = exchanged(outgoing.reshape(blocks), in_own[STRIPE // 2 :])
+    made = experts(rows, in_own, in_one, in_two, out_own)
+    (back,) = exchanged(made.reshape(blocks))
+    mixed = combine(back.reshape(EXPERTS, 4, CAP, 8, 128), spread)
+    return (attended[None], mixed[None])
 
 
 def solution(mesh):

time: 462 us -> 350 us (0.76)
  waiting for transfers between devices: 62.8 us -> 0 us
  local copies, waits for them, and re-layouts: 48.5 us -> 12.8 us
  Pallas kernels: 318 us -> 336 us
  between operations: 14.2 us -> 0.74 us
  other arithmetic: 8.23 us -> 0 us
  matrix products: 7.03 us -> 0 us
    all_gather x1 -> x0, waiting for transfers between devices: 62.1 us -> none  [attention(): piece = lax.all_gather(keys_values, 'ctx', axis=1, tiled=True)]
    pallas_call x0 -> x2, Pallas kernels: none -> 47.8 us  [the longest x1 44.3 us: attention(): pl.pallas_call(attention_kernel, out_shape=[jax.ShapeDtypeStruct((TOK, D)...]
    pallas_call x2, Pallas kernels: 175 us -> 149 us  [exchanged(): pl.pallas_call(exchange_kernel, out_shape=shapes, in_specs=[vmem] * len(g...]
    unnamed x31 -> x26, local copies, waits for them, and re-layouts: 22.5 us -> 7.93 us
    dot_general x5 -> x0, matrix products: 7.03 us -> none  [the longest x1 3.4 us: compute(): jnp.einsum('kgqn,nkh->kgqh', weights.astype(jnp.bfloat16), vals, preferre...]
    reshape x3 -> x0, local copies, waits for them, and re-layouts: 6 us -> none  [the longest x2 5.59 us: local(): back.reshape(N_EXP, 2, 4, CAP, 8, 128).transpose(0, 1, 3, 2, 4, 5)]
    another operation x1 -> x0, local copies, waits for them, and re-layouts: 5.08 us -> none  [experts(): rows.reshape(2, COUNT // PACK, BLOCK, PART)]
    reduce_sum x3 -> x0, other arithmetic: 5.05 us -> none  [the longest x1 2.19 us: local(): jnp.mean(values * values, axis=-1, keepdims=True) + 1e-06]
  transfers between devices with their start and end apart: 2 -> 0, of which waited for: 1 -> 0; matrix products, arithmetic and copies ran while one was open for 10% -> 0% of each run, Pallas kernels for 23% -> 0%
where the time goes in v3:
time: 350 us
  Pallas kernels  336 us (96%)
  local copies, waits for them, and re-layouts  12.8 us (4%)
    pallas_call x2, Pallas kernels, exchanged(): pl.pallas_call(exchange_kernel, out_shape=shapes, in_specs=[vmem] * len(g...  149 us
    pallas_call x1, Pallas kernels, experts(): pl.pallas_call(expert_kernel, out_shape=jax.ShapeDtypeStruct((2, COUNT //...  140 us
    pallas_call x1, Pallas kernels, attention(): pl.pallas_call(attention_kernel, out_shape=[jax.ShapeDtypeStruct((TOK, D)...  44.3 us
    unnamed x26, local copies, waits for them, and re-layouts  7.93 us

profile of v3, /device:TPU:1, one launch (start us, length us, event | category | flops | bytes accessed | tf_op | source)
XLA Modules:
  0.0 349.6 jit_solution(11066956553217981814)
XLA Ops:
  0.6 4.9 %fusion = (bf16[1,256,2,1536]{3,2,1,0:T(2,128)(2,1)}, bf16[1,256,2,1536]{3,2,1,0:T(2,128)(2,1)S(1)}) fusion(bf16[1,512,2,1536]{3,2,1,0:T(2,128)(2,1)} %param.12), kind=kLoop, calls=%fused_computation | loop fusion | bytes 6291456 | tf_op jit(solution)/shard_map/slice | solution.py:512
  5.5 0.0 copy-start.8
  5.5 0.0 copy-start.9
  5.5 0.0 copy-start.3
  5.5 0.0 copy-start.4
  5.5 0.0 copy-start.5
  5.5 0.2 copy.11
  5.7 0.4 copy-done.8
  6.2 0.1 copy.9
  6.3 0.0 copy-done.9
  6.3 0.1 copy.10
  6.4 0.4 copy-done.3
  6.7 0.0 copy-done.4
  6.8 0.0 copy-done.5
  6.8 0.0 copy-start.7
  6.8 44.3 %attention.1 = (bf16[128,4096]{1,0:T(8,128)(2,1)S(1)}, bf16[32,4,9,8,128]{4,3,2,1,0:T(8,128)(2,1)S(1)}, bf16[256,288]{1,0:T(8,128)(2,1)S(1)}, bf16[256,3072]{1,0:T(8,128)(2,1)S(1)}) custom-call(bf16[128,4096]{1,0:T(8,128)(2,1)S(1)} %bitcast.31, bf16[128,512]{1,0:T(8,128)(2,1)S(1)} %bitcast.32, f32[1,4096]{1,0:T(1,128)S(1)} %bitcast.33, ...), custom_call_target="tpu_custom_call" | custom-call | flops 4294967296 | bytes 8388608 | tf_op jit(solution)/shard_map/attention/pallas_call | solution.py:454
  51.1 0.0 copy-done.7
  51.1 0.2 copy.12
  51.3 0.0 copy-start.6
  51.3 76.1 %dispatch.1 = (bf16[128,9,8,128]{3,2,1,0:T(8,128)(2,1)S(1)}, bf16[256,3072]{1,0:T(8,128)(2,1)S(1)}) custom-call(bf16[128,9,8,128]{3,2,1,0:T(8,128)(2,1)S(1)} %bitcast.24, bf16[256,3072]{1,0:T(8,128)(2,1)S(1)} %bitcast.22), custom_call_target="tpu_custom_call" | custom-call | bytes 16777216 | tf_op jit(solution)/shard_map/dispatch/pallas_call | solution.py:265
  127.4 0.0 copy-start.1
  127.4 1.5 copy-done.1
  128.9 0.0 copy-done.6
  128.9 0.0 copy-start.2
  128.9 2.4 copy.13
  131.3 0.0 copy-done.2
  131.3 139.8 %experts.1 = bf16[2,4,16,9,8,128]{5,4,3,2,1,0:T(8,128)(2,1)} custom-call(bf16[2,4,16,9,8,128]{5,4,3,2,1,0:T(8,128)(2,1)} %bitcast.29, bf16[512,3072]{1,0:T(8,128)(2,1)} %bitcast.37, bf16[256,3072]{1,0:T(8,128)(2,1)S(1)} %get-tuple-element.11.in_one, bf16[256,3072]{1,0:T(8,128)(2,1)S(1)} %get-tuple-element.12.in_two, bf16[1536,512]{1,0:T(8,128)(2,1)S(1)} %bitcast.30), custom_call_target="tpu_custom_call" | custom-call | flops 10871635968 | bytes 14680064 | tf_op jit(solution)/shard_map/experts/pallas_call | solution.py:179
  271.0 0.0 copy-start
  271.1 1.7 copy-done
  272.7 72.4 %giveback.1 = bf16[128,9,8,128]{3,2,1,0:T(8,128)(2,1)S(1)} custom-call(bf16[128,9,8,128]{3,2,1,0:T(8,128)(2,1)S(1)} %bitcast.23), custom_call_target="tpu_custom_call" | custom-call | bytes 16777216 | tf_op jit(solution)/shard_map/giveback/pallas_call | solution.py:265
  345.2 3.5 combine.1
  348.6 1.0 copy.15
Async XLA Ops:
  5.5 0.7 copy-start.8
  5.5 0.8 copy-start.9
  5.5 1.3 copy-start.3
  5.5 1.3 copy-start.4
  5.5 1.2 copy-start.5
  6.8 44.3 %copy-start.7 = (bf16[1,256,2,1536]{3,2,1,0:T(2,128)(2,1)S(1)}, bf16[1,256,2,1536]{3,2,1,0:T(2,128)(2,1)}, u32[]{:S(2)}) copy-start(bf16[1,256,2,1536]{3,2,1,0:T(2,128)(2,1)} %get-tuple-element.14) | copy-start | bytes 4718596
  51.3 77.6 %copy-start.6 = (bf16[1,512,2,1536]{3,2,1,0:T(2,128)(2,1)S(1)}, bf16[1,512,2,1536]{3,2,1,0:T(2,128)(2,1)}, u32[]{:S(2)}) copy-start(bf16[1,512,2,1536]{3,2,1,0:T(2,128)(2,1)} %param.12) | copy-start | bytes 9437188
  127.4 1.5 copy-start.1
  128.9 2.4 copy-start.2
  271.0 1.7 copy-start

commit v4 on v1

v4 whole, which is shorter than its diff:
```python
import functools
import math

import jax
import jax.numpy as jnp
from jax import lax
from jax.experimental import pallas as pl
from jax.experimental.pallas import tpu as pltpu
from jax.sharding import PartitionSpec as P

D = 4096
FF = 1536
HEAD = 128
TOP = 8
QH = 32
KVH = 2
GROUP = 8
CAP = 9
EXPERTS = 32
TOK = 128
SLOTS = EXPERTS * CAP
N_EXP = 16
N_Z = 8
ROWS = N_EXP * N_Z * CAP
HALF = ROWS // 2
CHUNK = 16
COUNT = HALF // CHUNK
PACK = 9
BLOCK = CHUNK * PACK
LAG = 2
AHEAD = 4
TILE = 512
PART = D // 4
STRIPE = D // GROUP
GATHER = BLOCK // CAP


def block_kernel(q_ref, kv_ref, gain_ref, routing_ref, gate_ref, in_own, out_own, att_ref, mixed_ref,
                 qs, kv, acc, top, normed, broad, spread, columns, give, take, made_rows, back, in_oth, out_oth, part, recv, hid, flat, xb,
                 near, sends, recvs, w_sems, keep, d_send, d_recv, r_sems, s_send, s_recv, h_send, h_recv):
    c = lax.axis_index("ctx")
    e = lax.axis_index("exp")
    side, z = c % 2, c // 2
    core, x, y = e % 2, (e // 2) % 4, e // 8
    place = z % 4
    home = place * EXPERTS + 2 * e + z // 4
    mate = c + 1 - 2 * side

    def to(target):
        return dict(device_id={"ctx": target}, device_id_type=pl.DeviceIdType.MESH)

    def at(pe, pz):
        return dict(device_id={"exp": pe, "ctx": 2 * pz + side}, device_id_type=pl.DeviceIdType.MESH)

    def ahead(rel):
        return (y + rel // 8) % 2 * 8 + (x + (rel // 2) % 4) % 4 * 2 + (core + rel % 2) % 2

    def behind(rel):
        return (y + rel // 8) % 2 * 8 + (x + 4 - (rel // 2) % 4) % 4 * 2 + (core + rel % 2) % 2

    def turn(u):
        return (z + jnp.where(u % 2 == 1, (u + 1) // 2, N_Z - u // 2)) % N_Z

    def ring(way, d, which, block):
        target = jnp.where(way == 0, (z + 1) % N_Z, (z + N_Z - 1) % N_Z) * 2 + side
        return pltpu.make_async_remote_copy(
            src_ref=kv.at[block], dst_ref=kv.at[block], send_sem=sends.at[way, d, which], recv_sem=recvs.at[block], **to(target))

    def arrived(block):
        pltpu.make_async_remote_copy(
            src_ref=kv.at[block], dst_ref=kv.at[block], send_sem=near.at[0], recv_sem=recvs.at[block], **to(mate)).wait_recv()

    pair = pltpu.make_async_remote_copy(
        src_ref=kv.at[c], dst_ref=kv.at[c], send_sem=near.at[0], recv_sem=recvs.at[c], **to(mate))
    weights = pltpu.make_async_remote_copy(
        src_ref=in_own, dst_ref=in_oth, send_sem=w_sems.at[0], recv_sem=w_sems.at[1], **to(mate))
    down = pltpu.make_async_remote_copy(
        src_ref=out_own, dst_ref=out_oth, send_sem=w_sems.at[2], recv_sem=w_sems.at[3], **to(mate))

    barrier = pltpu.get_barrier_semaphore()
    pl.semaphore_signal(barrier, inc=1, **to(mate))

    def greet(o, _):
        pl.semaphore_signal(barrier, inc=1, **at(ahead(o // N_Z), (z + o) % N_Z))
        return 0

    lax.fori_loop(1, N_EXP * N_Z, greet, 0)
    kv[c] = kv_ref[...]
    pl.semaphore_wait(barrier, N_EXP * N_Z)
    pair.start()
    ring(0, 0, 0, c).start()
    ring(1, 0, 0, c).start()

    for h in range(QH):
        qs[pl.ds(h * TOK, TOK), :] = q_ref[:, h * HEAD : (h + 1) * HEAD]

    lanes = lax.broadcasted_iota(jnp.int32, (TOK, 128), 1)
    hit = jnp.zeros((TOK, 128), jnp.float32)
    gates = jnp.zeros((TOK, 128), jnp.float32)
    lanes = lanes.astype(jnp.float32)
    routes = routing_ref[...].astype(jnp.float32).T
    factors = gate_ref[...].T
    for k in range(TOP):
        same = (routes[:, k : k + 1] == lanes) & (lanes < EXPERTS)
        hit = jnp.where(same, 1.0, hit)
        gates = jnp.where(same, factors[:, k : k + 1], gates)
    earlier = lax.broadcasted_iota(jnp.int32, (TOK, TOK), 0) > lax.broadcasted_iota(jnp.int32, (TOK, TOK), 1)
    earlier = jnp.where(earlier, 1.0, 0.0).astype(jnp.bfloat16)
    slot = jnp.dot(earlier, hit.astype(jnp.bfloat16), preferred_element_type=jnp.float32)
    expert = lax.broadcasted_iota(jnp.int32, (128, SLOTS), 0)
    column = lax.broadcasted_iota(jnp.int32, (128, SLOTS), 1)
    begin = expert * CAP
    widen = jnp.where((column >= begin) & (column < begin + CAP), 1.0, 0.0).astype(jnp.bfloat16)

    def wide(part):
        return jnp.dot(part.astype(jnp.bfloat16), widen, preferred_element_type=jnp.float32)

    inside = jnp.where((column >= begin) & (column < begin + CAP), column - begin, 0).astype(jnp.float32)
    number = jnp.sum(inside, axis=0, keepdims=True)
    chosen = (wide(hit) > 0.5) & (wide(slot) == number)
    high = gates.astype(jnp.bfloat16).astype(jnp.float32)
    spread[0:TOK, :] = jnp.where(chosen, wide(high), 0.0).astype(jnp.bfloat16)
    spread[TOK : 2 * TOK, :] = jnp.where(chosen, wide(gates - high), 0.0).astype(jnp.bfloat16)
    pick = jnp.where(chosen, 1.0, 0.0).T.astype(jnp.bfloat16)

    arrived(mate)
    ring(0, 0, 1, mate).start()
    ring(1, 0, 1, mate).start()
    weights.start()

    scale = math.log2(math.e) / math.sqrt(HEAD)
    chunk = 2 * TOK

    def attend(zk, diagonal):
        for g in range(KVH):
            keys = kv[pl.ds(2 * zk, 2), :, g * HEAD : (g + 1) * HEAD].reshape(2 * TOK, HEAD)
            vals = kv[pl.ds(2 * zk, 2), :, (KVH + g) * HEAD : (KVH + g + 1) * HEAD].reshape(2 * TOK, HEAD)
            vals = jnp.concatenate([vals, jnp.ones((2 * TOK, HEAD), jnp.bfloat16)], axis=1)

            def rows(n, _):
                here = pl.ds(pl.multiple_of(g * (QH // KVH) * TOK + n * chunk, chunk), chunk)
                score = scale * lax.dot_general(qs[here, :], keys, (((1,), (1,)), ((), ())), preferred_element_type=jnp.float32)
                if diagonal:
                    token = lax.broadcasted_iota(jnp.int32, (chunk, 2 * TOK), 0) % TOK
                    place = lax.broadcasted_iota(jnp.int32, (chunk, 2 * TOK), 1)
                    score = jnp.where(place <= token + TOK * side, score, -1e30)
                    newest = jnp.broadcast_to(jnp.max(score, axis=1, keepdims=True), (chunk, HEAD))
                else:
                    before = top[here, :]
                    newest = jnp.maximum(before, jnp.max(score, axis=1, keepdims=True))
                probs = jnp.exp2(score - jnp.concatenate([newest, newest], axis=1)).astype(jnp.bfloat16)
                made = jnp.dot(probs, vals, preferred_element_type=jnp.float32)
                if not diagonal:
                    keep = jnp.exp2(before - newest)
                    made += acc[here, :] * jnp.concatenate([keep, keep], axis=1)
                acc[here, :] = made
                top[here, :] = newest
                return 0

            lax.fori_loop(0, QH // KVH * TOK // chunk, rows, 0, unroll=2)

    attend(z, True)

    def stage(d, _):
        low, up = (z + N_Z - d) % N_Z, (z + d) % N_Z

        @pl.when(d < 4)
        def _():
            def one(w, _):
                v = (side + w) % 2
                arrived(2 * low + v)

                @pl.when((d < 3) | (v == 0))
                def _():
                    ring(0, d, w, 2 * low + v).start()
                arrived(2 * up + v)

                @pl.when((d < 3) | (v == 1))
                def _():
                    ring(1, d, w, 2 * up + v).start()
                return 0
            lax.fori_loop(0, 2, one, 0)

        @pl.when(d == 4)
        def _():
            arrived(2 * up)
            arrived(2 * up + 1)

        def way(w, _):
            zk = jnp.where(w == 0, low, up)

            @pl.when((zk < z) & ((d < 4) | (w == 0)))
            def _():
                attend(zk, False)
            return 0
        lax.fori_loop(0, 2, way, 0)
        return 0

    lax.fori_loop(1, 5, stage, 0)

    squares = jnp.zeros((TOK, HEAD), jnp.float32)
    for h in range(QH):
        here = pl.ds(h * TOK, TOK)
        out = (acc[here, 0:HEAD] / acc[here, HEAD : 2 * HEAD]).astype(jnp.bfloat16)
        att_ref[:, h * HEAD : (h + 1) * HEAD] = out
        out = out.astype(jnp.float32)
        squares += out * out
    root = lax.rsqrt(jnp.sum(squares, axis=1, keepdims=True) / D + 1e-06)
    for h in range(QH):
        cols = slice(h * HEAD, (h + 1) * HEAD)
        normed[:, cols] = (att_ref[:, cols].astype(jnp.float32) * root * gain_ref[:, cols]).astype(jnp.bfloat16)
    for n in range(4):
        cols = slice(n * PART, (n + 1) * PART)
        picked = jnp.dot(pick, normed[:, cols], preferred_element_type=jnp.float32)
        for k in range(8):
            broad[pl.ds(k, SLOTS, stride=8), :] = picked[:, k * 128 : (k + 1) * 128]
        give[n * EXPERTS : (n + 1) * EXPERTS] = broad[...].astype(jnp.bfloat16).reshape(EXPERTS, CAP, 8, 128)

    own = pl.ds(pl.multiple_of(side * STRIPE, STRIPE), STRIPE)
    oth = pl.ds(pl.multiple_of((1 - side) * STRIPE, STRIPE), STRIPE)

    def sum_copy(d, i):
        target = jnp.where(d == 1, c + 2, c - 2)
        return pltpu.make_async_remote_copy(
            src_ref=part.at[d, i], dst_ref=recv.at[d, i], send_sem=s_send.at[d, i], recv_sem=s_recv.at[d, i],
            device_id={"ctx": target}, device_id_type=pl.DeviceIdType.MESH)

    def hid_copy(d, i):
        target = jnp.where(d == 1, c - 2, c + 2)
        return pltpu.make_async_remote_copy(
            src_ref=hid.at[d, i], dst_ref=hid.at[d, i], send_sem=h_send.at[d, i], recv_sem=h_recv.at[d, i],
            device_id={"ctx": target}, device_id_type=pl.DeviceIdType.MESH)

    def products(d, b):
        flat[...] = take[d, b].astype(jnp.float32).reshape(8 * BLOCK, 128)
        for k in range(8):
            xb[:, k * 128 : (k + 1) * 128] = flat[pl.ds(k, BLOCK, stride=8), :].astype(jnp.bfloat16)

        def tile(n, _):
            cols = pl.ds(pl.multiple_of(n * TILE, TILE), TILE)
            made = jnp.dot(xb[:, own], in_own[:, cols], preferred_element_type=jnp.float32)
            made += jnp.dot(xb[:, oth], in_oth[:, cols], preferred_element_type=jnp.float32)
            part[d, pl.ds(b * PACK, PACK), :, cols] = made.astype(jnp.bfloat16).reshape(PACK, CHUNK, TILE)
            return 0
        lax.fori_loop(0, 2 * FF // TILE, tile, 0)

    def result(d, b):
        rows = hid[d, pl.ds(b * PACK, PACK)].reshape(BLOCK, FF)
        mine = jnp.dot(rows, out_own[...], preferred_element_type=jnp.float32)
        theirs = jnp.dot(rows, out_oth[...], preferred_element_type=jnp.float32)
        for k in range(4):
            cols = slice(k * 128, (k + 1) * 128)
            flat[pl.ds(k, BLOCK, stride=8), :] = jnp.where(side == 0, mine[:, cols], theirs[:, cols])
            flat[pl.ds(k + 4, BLOCK, stride=8), :] = jnp.where(side == 0, theirs[:, cols], mine[:, cols])
        made_rows[d, b] = flat[...].astype(jnp.bfloat16).reshape(GATHER, CAP, 8, 128)

        def back_home(j, _):
            low, s = j // N_Z, turn(j % N_Z)
            rel = d * 8 + 2 * b + low
            local = (rel == 0) & (j == 0)

            @pl.when(local)
            def _():
                pltpu.make_async_copy(made_rows.at[0, 0, z], back.at[home], keep.at[1]).start()

            @pl.when(jnp.logical_not(local))
            def _():
                pltpu.make_async_remote_copy(
                    src_ref=made_rows.at[d, b, low * N_Z + s], dst_ref=back.at[home], send_sem=r_sems.at[0], recv_sem=r_sems.at[1],
                    **at(behind(rel), s)).start()
            return 0

        lax.fori_loop(0, GATHER, back_home, 0)

    def dispatch(b, u):
        pz = turn(u)

        def one(v, _):
            d, low = v % 2, v // 2
            rel = d * 8 + 2 * b + low
            pe = ahead(rel)
            local = (rel == 0) & (u == 0)

            @pl.when(local)
            def _():
                pltpu.make_async_copy(give.at[home], take.at[0, 0, z], keep.at[0]).start()

            @pl.when(jnp.logical_not(local))
            def _():
                pltpu.make_async_remote_copy(
                    src_ref=give.at[pz % 4 * EXPERTS + 2 * pe + pz // 4], dst_ref=take.at[d, b, low * N_Z + z],
                    send_sem=d_send.at[0], recv_sem=d_recv.at[d, b], **at(pe, pz)).start()
            return 0

        lax.fori_loop(0, 4, one, 0)

    def ahead_of_time(n, _):
        dispatch(n // N_Z, n % N_Z)
        return 0

    lax.fori_loop(0, AHEAD * N_Z, ahead_of_time, 0)
    down.start()

    def await_rows(d, b, count):
        pltpu.make_async_remote_copy(
            src_ref=take.at[d, b, pl.ds(0, count)], dst_ref=take.at[d, b, pl.ds(0, count)], send_sem=d_send.at[0],
            recv_sem=d_recv.at[d, b], **to(mate)).wait_recv()

    def step(t, _):
        @pl.when((t // PACK + AHEAD < COUNT // PACK) & (t % PACK < N_Z))
        def _():
            dispatch(t // PACK + AHEAD, t % PACK)

        @pl.when((t % PACK == 0) & (t < COUNT))
        def _():
            @pl.when(t == 0)
            def _():
                weights.wait_recv()
                pltpu.make_async_copy(give.at[home], take.at[0, 0, z], keep.at[0]).wait()
                await_rows(0, 0, GATHER - 1)

            @pl.when(t > 0)
            def _():
                await_rows(0, t // PACK, GATHER)

            def both(d, _):
                @pl.when(d == 1)
                def _():
                    await_rows(1, t // PACK, GATHER)
                products(d, t // PACK)
                return 0
            lax.fori_loop(0, 2, both, 0)

        @pl.when(t == 3 * LAG + PACK - 1)
        def _():
            down.wait_recv()

        def direction(d, _):
            pos = jnp.where(d == 1, place, 3 - place)
            i = t - LAG * pos

            @pl.when((i >= 0) & (i < COUNT))
            def _():
                @pl.when(pos == 0)
                def _():
                    sum_copy(d, i).start()

                @pl.when((pos > 0) & (pos < 3))
                def _():
                    sum_copy(d, i).wait_recv()
                    part[d, i] = (part[d, i].astype(jnp.float32) + recv[d, i].astype(jnp.float32)).astype(jnp.bfloat16)
                    sum_copy(d, i).start()

                @pl.when(pos == 3)
                def _():
                    sum_copy(d, i).wait_recv()
                    total = part[d, i].astype(jnp.float32) + recv[d, i].astype(jnp.float32)
                    gate = total[:, :FF]
                    hid[d, i] = (jax.nn.silu(gate) * total[:, FF:]).astype(jnp.bfloat16)
                    hid_copy(d, i).start()

            k = t - 3 * LAG - LAG * (3 - pos)

            @pl.when((k >= 0) & (k < COUNT))
            def _():
                @pl.when(pos < 3)
                def _():
                    hid_copy(d, k).wait_recv()

                @pl.when((pos > 0) & (pos < 3))
                def _():
                    hid_copy(d, k).start()

                @pl.when(k % PACK == PACK - 1)
                def _():
                    result(d, k // PACK)
            return 0

        lax.fori_loop(0, 2, direction, 0)
        return 0

    lax.fori_loop(0, COUNT + 6 * LAG, step, 0)

    def drain(i, _):
        def direction(d, _):
            pos = jnp.where(d == 1, place, 3 - place)

            @pl.when(pos < 3)
            def _():
                sum_copy(d, i).wait_send()

            @pl.when(pos > 0)
            def _():
                hid_copy(d, i).wait_send()
            return 0
        lax.fori_loop(0, 2, direction, 0)
        return 0

    lax.fori_loop(0, COUNT, drain, 0)
    weights.wait_send()
    down.wait_send()
    pltpu.make_async_copy(made_rows.at[0, 0, z], back.at[home], keep.at[1]).wait()
    others = pl.ds(0, N_EXP * N_Z - 1)
    pltpu.make_async_remote_copy(
        src_ref=give.at[others], dst_ref=back.at[others], send_sem=d_send.at[0], recv_sem=r_sems.at[1], **to(mate)).wait_send()
    returned = pltpu.make_async_remote_copy(
        src_ref=back.at[others], dst_ref=back.at[others], send_sem=r_sems.at[0], recv_sem=r_sems.at[1], **to(mate))
    returned.wait_send()
    returned.wait_recv()

    def quarter(n, _):
        broad[...] = back[pl.ds(n * EXPERTS, EXPERTS)].astype(jnp.float32).reshape(8 * SLOTS, 128)
        for k in range(8):
            columns[:, k * 128 : (k + 1) * 128] = broad[pl.ds(k, SLOTS, stride=8), :].astype(jnp.bfloat16)
        total = jnp.dot(spread[...], columns[...], preferred_element_type=jnp.float32)
        mixed_ref[:, pl.ds(pl.multiple_of(n * PART, PART), PART)] = (total[:TOK] + total[TOK:]).astype(jnp.bfloat16)
        return 0

    lax.fori_loop(0, 4, quarter, 0)

    pair.wait_send()

    def drain(d, _):
        def one(w, _):
            v = (side + w) % 2

            @pl.when((d < 3) | (v == 0))
            def _():
                ring(0, d, w, c).wait_send()

            @pl.when((d < 3) | (v == 1))
            def _():
                ring(1, d, w, c).wait_send()
            return 0
        return lax.fori_loop(0, 2, one, 0)

    lax.fori_loop(0, 4, drain, 0)


def block(queries, keys_values, gain, routing, gate_weights, in_own, out_own):
    vmem = pl.BlockSpec(memory_space=pltpu.VMEM)
    blocks = (N_EXP * N_Z, CAP, 8, 128)
    grouped = (2, COUNT // PACK, GATHER, CAP, 8, 128)
    bf16 = jnp.bfloat16
    return pl.pallas_call(
        block_kernel,
        out_shape=[jax.ShapeDtypeStruct((TOK, D), bf16), jax.ShapeDtypeStruct((TOK, D), bf16)],
        in_specs=[vmem] * 7,
        out_specs=[vmem] * 2,
        scratch_shapes=[
            pltpu.VMEM((QH * TOK, HEAD), bf16),
            pltpu.VMEM((2 * N_Z, TOK, 2 * KVH * HEAD), bf16),
            pltpu.VMEM((QH * TOK, 2 * HEAD), jnp.float32),
            pltpu.VMEM((QH * TOK, HEAD), jnp.float32),
            pltpu.VMEM((TOK, D), bf16),
            pltpu.VMEM((8 * SLOTS, 128), jnp.float32),
            pltpu.VMEM((2 * TOK, SLOTS), bf16),
            pltpu.VMEM((SLOTS, PART), bf16),
            pltpu.VMEM(blocks, bf16),
            pltpu.VMEM(grouped, bf16),
            pltpu.VMEM(grouped, bf16),
            pltpu.VMEM(blocks, bf16),
            pltpu.VMEM((STRIPE, 2 * FF), bf16),
            pltpu.VMEM((FF, STRIPE), bf16),
            pltpu.VMEM((2, COUNT, CHUNK, 2 * FF), bf16),
            pltpu.VMEM((2, COUNT, CHUNK, 2 * FF), bf16),
            pltpu.VMEM((2, COUNT, CHUNK, FF), bf16),
            pltpu.VMEM((8 * BLOCK, 128), jnp.float32),
            pltpu.VMEM((BLOCK, PART), bf16),
            pltpu.SemaphoreType.DMA((1,)),
            pltpu.SemaphoreType.DMA((2, 4, 2)),
            pltpu.SemaphoreType.DMA((2 * N_Z,)),
            pltpu.SemaphoreType.DMA((4,)),
            pltpu.SemaphoreType.DMA((2,)),
            pltpu.SemaphoreType.DMA((1,)),
            pltpu.SemaphoreType.DMA((2, COUNT // PACK)),
            pltpu.SemaphoreType.DMA((2,)),
            pltpu.SemaphoreType.DMA((2, COUNT)),
            pltpu.SemaphoreType.DMA((2, COUNT)),
            pltpu.SemaphoreType.DMA((2, COUNT)),
            pltpu.SemaphoreType.DMA((2, COUNT)),
        ],
        compiler_params=pltpu.CompilerParams(collective_id=1, has_side_effects=True, vmem_limit_bytes=60 * 2**20),
        cost_estimate=pl.CostEstimate(flops=26 * 10**9, bytes_accessed=12 * 2**20, transcendentals=TOK * 2048 * QH),
        name="block",
    )(queries, keys_values, gain, routing, gate_weights, in_own, out_own)


def local(queries, keys_values, norm_gain, routing, gate_weights, expert_in, expert_out):
    in_own = expert_in[0].reshape(STRIPE, 2 * FF)
    attended, mixed = block(
        queries[0], keys_values[0], norm_gain[None], routing[0].T, gate_weights[0].T, in_own, expert_out[0])
    return (attended[None], mixed[None])


def solution(mesh):
    in_specs = (
        P("exp", "ctx", None),
        P("exp", "ctx", None),
        P(),
        P("exp", "ctx", None),
        P("exp", "ctx", None),
        P(("exp", "ctx"), None, None, None),
        P(("exp", "ctx"), None, None),
    )
    out_specs = (P("exp", "ctx", None), P("exp", "ctx", None))
    return jax.shard_map(local, mesh=mesh, in_specs=in_specs, out_specs=out_specs, check_vma=False)
```

time: 525 us -> 322 us (0.61)
  waiting for transfers between devices: 214 us -> 0 us
  Pallas kernels: 137 us -> 313 us
  blocking collectives: 50.4 us -> 0 us
  starting transfers between devices: 48 us -> 0 us
  local copies, waits for them, and re-layouts: 45.2 us -> 8.88 us
  between operations: 14.3 us -> 0.64 us
  other arithmetic: 7.3 us -> 0 us
  matrix products: 7.02 us -> 0 us
    pallas_call x1, Pallas kernels: 137 us -> 313 us  [block(): pl.pallas_call(block_kernel, out_shape=[jax.ShapeDtypeStruct((TOK, D), bf...]
    all_to_all x3 -> x0, waiting for transfers between devices: 86.5 us -> none  [the longest x2 86.5 us: along_z(): lax.all_to_all(array, 'ctx', split_axis=0, concat_axis=0, axis_index_grou...]
    all_gather x1 -> x0, waiting for transfers between devices: 66.8 us -> none  [attention(): piece = lax.all_gather(keys_values, 'ctx', axis=1, tiled=True)]
    ppermute x2 -> x0, waiting for transfers between devices: 60.2 us -> none  [paired(): return lax.ppermute(array, 'ctx', [(i, i ^ 1) for i in range(16)])]
    all_to_all x1 -> x0, blocking collectives: 50.4 us -> none  [along_exp(): return lax.all_to_all(array, 'exp', split_axis=0, concat_axis=0, tiled=True)]
    all_to_all x3 -> x0, starting transfers between devices: 47.1 us -> none  [the longest x2 32.2 us: along_z(): lax.all_to_all(array, 'ctx', split_axis=0, concat_axis=0, axis_index_grou...]
    reshape x5 -> x0, local copies, waits for them, and re-layouts: 14.1 us -> none  [the longest x2 6.85 us: local(): outgoing.astype(jnp.bfloat16).reshape(2, N_EXP * CAP, 4, PART)]
    dot_general x5 -> x0, matrix products: 7.02 us -> none  [the longest x1 3.4 us: compute(): jnp.einsum('kgqn,nkh->kgqh', weights.astype(jnp.bfloat16), vals, preferre...]
  transfers between devices with their start and end apart: 6 -> 0, of which waited for: 4 -> 0; matrix products, arithmetic and copies ran while one was open for 5% -> 0% of each run, Pallas kernels for 0% -> 0%
where the time goes in v4:
time: 322 us
  Pallas kernels  313 us (97%)
  local copies, waits for them, and re-layouts  8.88 us (3%)
    pallas_call x1, Pallas kernels, block(): pl.pallas_call(block_kernel, out_shape=[jax.ShapeDtypeStruct((TOK, D), bf...  313 us
    unnamed x3, local copies, waits for them, and re-layouts  8.88 us

profile of v4, /device:TPU:1, one launch (start us, length us, event | category | flops | bytes accessed | tf_op | source)
XLA Modules:
  0.0 322.2 jit_solution(16273536104855327343)
XLA Ops:
  0.6 4.3 %copy.9 = bf16[64,8,2,1536]{3,1,2,0:T(8,128)(2,1)} copy(bf16[64,8,2,1536]{3,2,1,0:T(2,128)(2,1)} %bitcast.15) | data formatting | bytes 6291456
  4.9 312.7 %block.1 = (bf16[128,4096]{1,0:T(8,128)(2,1)}, bf16[128,4096]{1,0:T(8,128)(2,1)}) custom-call(bf16[128,4096]{1,0:T(8,128)(2,1)} %bitcast.20, bf16[128,512]{1,0:T(8,128)(2,1)} %bitcast.21, f32[1,4096]{1,0:T(1,128)} %bitcast.22, s32[8,128]{1,0:T(8,128)} %bitcast.23, f32[8,128]{1,0:T(8,128)} %bitcast.24, bf16[512,3072]{1,0:T(8,128)(2,1)} %bitcast.16, ...), custom_call_target="tpu_custom_call" | custom-call | flops 25999998976 | bytes 12582912 | tf_op jit(solution)/shard_map/block/pallas_call | solution.py:445
  317.7 2.3 copy.12
  320.0 2.3 copy.13

commit v5 on v4

--- a/solution.py
+++ b/solution.py
@@ -28,6 +28,7 @@
 PACK = 9
 BLOCK = CHUNK * PACK
 LAG = 2
+BACK_LAG = 2
 AHEAD = 4
 TILE = 512
 PART = D // 4
@@ -35,8 +36,8 @@
 GATHER = BLOCK // CAP
 
 
-def block_kernel(q_ref, kv_ref, gain_ref, routing_ref, gate_ref, in_own, out_own, att_ref, mixed_ref,
-                 qs, kv, acc, top, normed, broad, spread, columns, give, take, made_rows, back, in_oth, out_oth, part, recv, hid, flat, xb,
+def block_kernel(q_ref, kv_ref, gain_ref, routing_ref, gate_ref, in_own, out_own, att_ref, back, spread,
+                 qs, kv, acc, top, normed, broad, give, take, made_rows, in_oth, out_oth, part, recv, hid, flat, xb,
                  near, sends, recvs, w_sems, keep, d_send, d_recv, r_sems, s_send, s_recv, h_send, h_recv):
     c = lax.axis_index("ctx")
     e = lax.axis_index("exp")
@@ -53,10 +54,10 @@
         return dict(device_id={"exp": pe, "ctx": 2 * pz + side}, device_id_type=pl.DeviceIdType.MESH)
 
     def ahead(rel):
-        return (y + rel // 8) % 2 * 8 + (x + (rel // 2) % 4) % 4 * 2 + (core + rel % 2) % 2
+        return (y + rel // 8) % 2 * 8 + (x + (rel // 2 + rel // 8 + rel % 2 * 2) % 4) % 4 * 2 + (core + rel % 2) % 2
 
     def behind(rel):
-        return (y + rel // 8) % 2 * 8 + (x + 4 - (rel // 2) % 4) % 4 * 2 + (core + rel % 2) % 2
+        return (y + rel // 8) % 2 * 8 + (x + 4 - (rel // 2 + rel // 8 + rel % 2 * 2) % 4) % 4 * 2 + (core + rel % 2) % 2
 
     def turn(u):
         return (z + jnp.where(u % 2 == 1, (u + 1) // 2, N_Z - u // 2)) % N_Z
@@ -90,6 +91,7 @@
     pair.start()
     ring(0, 0, 0, c).start()
     ring(1, 0, 0, c).start()
+    weights.start()
 
     for h in range(QH):
         qs[pl.ds(h * TOK, TOK), :] = q_ref[:, h * HEAD : (h + 1) * HEAD]
@@ -126,7 +128,6 @@
     arrived(mate)
     ring(0, 0, 1, mate).start()
     ring(1, 0, 1, mate).start()
-    weights.start()
 
     scale = math.log2(math.e) / math.sqrt(HEAD)
     chunk = 2 * TOK
@@ -161,6 +162,51 @@
 
     attend(z, True)
 
+    def finish():
+        squares = jnp.zeros((TOK, HEAD), jnp.float32)
+        for h in range(QH):
+            here = pl.ds(h * TOK, TOK)
+            out = (acc[here, 0:HEAD] / acc[here, HEAD : 2 * HEAD]).astype(jnp.bfloat16)
+            att_ref[:, h * HEAD : (h + 1) * HEAD] = out
+            out = out.astype(jnp.float32)
+            squares += out * out
+        root = lax.rsqrt(jnp.sum(squares, axis=1, keepdims=True) / D + 1e-06)
+        for h in range(QH):
+            cols = slice(h * HEAD, (h + 1) * HEAD)
+            normed[:, cols] = (att_ref[:, cols].astype(jnp.float32) * root * gain_ref[:, cols]).astype(jnp.bfloat16)
+        for n in range(4):
+            cols = slice(n * PART, (n + 1) * PART)
+            picked = jnp.dot(pick, normed[:, cols], preferred_element_type=jnp.float32)
+            for k in range(8):
+                broad[pl.ds(k, SLOTS, stride=8), :] = picked[:, k * 128 : (k + 1) * 128]
+            give[n * EXPERTS : (n + 1) * EXPERTS] = broad[...].astype(jnp.bfloat16).reshape(EXPERTS, CAP, 8, 128)
+
+    def dispatch(b, u):
+        pz = turn(u)
+
+        def one(v, _):
+            d, low = v % 2, v // 2
+            rel = d * 8 + 2 * b + low
+            pe = ahead(rel)
+            local = (rel == 0) & (u == 0)
+
+            @pl.when(local)
+            def _():
+                pltpu.make_async_copy(give.at[home], take.at[0, 0, z], keep.at[0]).start()
+
+            @pl.when(jnp.logical_not(local))
+            def _():
+                pltpu.make_async_remote_copy(
+                    src_ref=give.at[pz % 4 * EXPERTS + 2 * pe + pz // 4], dst_ref=take.at[d, b, low * N_Z + z],
+                    send_sem=d_send.at[0], recv_sem=d_recv.at[d, b], **at(pe, pz)).start()
+            return 0
+
+        lax.fori_loop(0, 4, one, 0)
+
+    def ahead_of_time(n, _):
+        dispatch(n // N_Z, n % N_Z)
+        return 0
+
     def stage(d, _):
         low, up = (z + N_Z - d) % N_Z, (z + d) % N_Z
 
@@ -194,27 +240,18 @@
                 attend(zk, False)
             return 0
         lax.fori_loop(0, 2, way, 0)
+
+        @pl.when(d == 4)
+        def _():
+            finish()
+
+        @pl.when(d == 4)
+        def _():
+            lax.fori_loop(0, AHEAD * N_Z, ahead_of_time, 0)
         return 0
 
     lax.fori_loop(1, 5, stage, 0)
-
-    squares = jnp.zeros((TOK, HEAD), jnp.float32)
-    for h in range(QH):
-        here = pl.ds(h * TOK, TOK)
-        out = (acc[here, 0:HEAD] / acc[here, HEAD : 2 * HEAD]).astype(jnp.bfloat16)
-        att_ref[:, h * HEAD : (h + 1) * HEAD] = out
-        out = out.astype(jnp.float32)
-        squares += out * out
-    root = lax.rsqrt(jnp.sum(squares, axis=1, keepdims=True) / D + 1e-06)
-    for h in range(QH):
-        cols = slice(h * HEAD, (h + 1) * HEAD)
-        normed[:, cols] = (att_ref[:, cols].astype(jnp.float32) * root * gain_ref[:, cols]).astype(jnp.bfloat16)
-    for n in range(4):
-        cols = slice(n * PART, (n + 1) * PART)
-        picked = jnp.dot(pick, normed[:, cols], preferred_element_type=jnp.float32)
-        for k in range(8):
-            broad[pl.ds(k, SLOTS, stride=8), :] = picked[:, k * 128 : (k + 1) * 128]
-        give[n * EXPERTS : (n + 1) * EXPERTS] = broad[...].astype(jnp.bfloat16).reshape(EXPERTS, CAP, 8, 128)
+    down.start()
 
     own = pl.ds(pl.multiple_of(side * STRIPE, STRIPE), STRIPE)
     oth = pl.ds(pl.multiple_of((1 - side) * STRIPE, STRIPE), STRIPE)
@@ -272,35 +309,6 @@
 
         lax.fori_loop(0, GATHER, back_home, 0)
 
-    def dispatch(b, u):
-        pz = turn(u)
-
-        def one(v, _):
-            d, low = v % 2, v // 2
-            rel = d * 8 + 2 * b + low
-            pe = ahead(rel)
-            local = (rel == 0) & (u == 0)
-
-            @pl.when(local)
-            def _():
-                pltpu.make_async_copy(give.at[home], take.at[0, 0, z], keep.at[0]).start()
-
-            @pl.when(jnp.logical_not(local))
-            def _():
-                pltpu.make_async_remote_copy(
-                    src_ref=give.at[pz % 4 * EXPERTS + 2 * pe + pz // 4], dst_ref=take.at[d, b, low * N_Z + z],
-                    send_sem=d_send.at[0], recv_sem=d_recv.at[d, b], **at(pe, pz)).start()
-            return 0
-
-        lax.fori_loop(0, 4, one, 0)
-
-    def ahead_of_time(n, _):
-        dispatch(n // N_Z, n % N_Z)
-        return 0
-
-    lax.fori_loop(0, AHEAD * N_Z, ahead_of_time, 0)
-    down.start()
-
     def await_rows(d, b, count):
         pltpu.make_async_remote_copy(
             src_ref=take.at[d, b, pl.ds(0, count)], dst_ref=take.at[d, b, pl.ds(0, count)], send_sem=d_send.at[0],
@@ -359,7 +367,7 @@
                     hid[d, i] = (jax.nn.silu(gate) * total[:, FF:]).astype(jnp.bfloat16)
                     hid_copy(d, i).start()
 
-            k = t - 3 * LAG - LAG * (3 - pos)
+            k = t - 3 * LAG - BACK_LAG * (3 - pos)
 
             @pl.when((k >= 0) & (k < COUNT))
             def _():
@@ -379,7 +387,7 @@
         lax.fori_loop(0, 2, direction, 0)
         return 0
 
-    lax.fori_loop(0, COUNT + 6 * LAG, step, 0)
+    lax.fori_loop(0, COUNT + 3 * LAG + 3 * BACK_LAG, step, 0)
 
     def drain(i, _):
         def direction(d, _):
@@ -408,16 +416,6 @@
     returned.wait_send()
     returned.wait_recv()
 
-    def quarter(n, _):
-        broad[...] = back[pl.ds(n * EXPERTS, EXPERTS)].astype(jnp.float32).reshape(8 * SLOTS, 128)
-        for k in range(8):
-            columns[:, k * 128 : (k + 1) * 128] = broad[pl.ds(k, SLOTS, stride=8), :].astype(jnp.bfloat16)
-        total = jnp.dot(spread[...], columns[...], preferred_element_type=jnp.float32)
-        mixed_ref[:, pl.ds(pl.multiple_of(n * PART, PART), PART)] = (total[:TOK] + total[TOK:]).astype(jnp.bfloat16)
-        return 0
-
-    lax.fori_loop(0, 4, quarter, 0)
-
     pair.wait_send()
 
     def drain(d, _):
@@ -444,9 +442,13 @@
     bf16 = jnp.bfloat16
     return pl.pallas_call(
         block_kernel,
-        out_shape=[jax.ShapeDtypeStruct((TOK, D), bf16), jax.ShapeDtypeStruct((TOK, D), bf16)],
+        out_shape=[
+            jax.ShapeDtypeStruct((TOK, D), bf16),
+            jax.ShapeDtypeStruct(blocks, bf16),
+            jax.ShapeDtypeStruct((2 * TOK, SLOTS), bf16),
+        ],
         in_specs=[vmem] * 7,
-        out_specs=[vmem] * 2,
+        out_specs=[vmem] * 3,
         scratch_shapes=[
             pltpu.VMEM((QH * TOK, HEAD), bf16),
             pltpu.VMEM((2 * N_Z, TOK, 2 * KVH * HEAD), bf16),
@@ -454,12 +456,9 @@
             pltpu.VMEM((QH * TOK, HEAD), jnp.float32),
             pltpu.VMEM((TOK, D), bf16),
             pltpu.VMEM((8 * SLOTS, 128), jnp.float32),
-            pltpu.VMEM((2 * TOK, SLOTS), bf16),
-            pltpu.VMEM((SLOTS, PART), bf16),
             pltpu.VMEM(blocks, bf16),
             pltpu.VMEM(grouped, bf16),
             pltpu.VMEM(grouped, bf16),
-            pltpu.VMEM(blocks, bf16),
             pltpu.VMEM((STRIPE, 2 * FF), bf16),
             pltpu.VMEM((FF, STRIPE), bf16),
             pltpu.VMEM((2, COUNT, CHUNK, 2 * FF), bf16),
@@ -486,10 +485,39 @@
     )(queries, keys_values, gain, routing, gate_weights, in_own, out_own)
 
 
+def combine_kernel(back_ref, spread_ref, att_ref, attended_ref, mixed_ref, broad, columns):
+    attended_ref[...] = att_ref[...]
+    broad[...] = back_ref[...].astype(jnp.float32).reshape(8 * SLOTS, 128)
+    for k in range(8):
+        columns[:, k * 128 : (k + 1) * 128] = broad[pl.ds(k, SLOTS, stride=8), :].astype(jnp.bfloat16)
+    total = jnp.dot(spread_ref[...], columns[...], preferred_element_type=jnp.float32)
+    mixed_ref[...] = (total[:TOK] + total[TOK:]).astype(jnp.bfloat16)
+
+
+def combine(back, spread, attended):
+    shape = jax.ShapeDtypeStruct((TOK, D), jnp.bfloat16)
+    columns = pl.BlockSpec((TOK, PART), lambda n: (0, n))
+    return pl.pallas_call(
+        combine_kernel,
+        grid=(4,),
+        out_shape=[shape, shape],
+        in_specs=[
+            pl.BlockSpec((EXPERTS, CAP, 8, 128), lambda n: (n, 0, 0, 0)),
+            pl.BlockSpec((2 * TOK, SLOTS), lambda n: (0, 0)),
+            columns,
+        ],
+        out_specs=[columns, columns],
+        scratch_shapes=[pltpu.VMEM((8 * SLOTS, 128), jnp.float32), pltpu.VMEM((SLOTS, PART), jnp.bfloat16)],
+        compiler_params=pltpu.CompilerParams(vmem_limit_bytes=24 * 2**20),
+        name="combine",
+    )(back, spread, attended)
+
+
 def local(queries, keys_values, norm_gain, routing, gate_weights, expert_in, expert_out):
     in_own = expert_in[0].reshape(STRIPE, 2 * FF)
-    attended, mixed = block(
+    attended, back, spread = block(
         queries[0], keys_values[0], norm_gain[None], routing[0].T, gate_weights[0].T, in_own, expert_out[0])
+    attended, mixed = combine(back, spread, attended)
     return (attended[None], mixed[None])
 
 

time: 322 us -> 321 us (level)
    pallas_call x1, Pallas kernels: 313 us -> 309 us  [block(): pl.pallas_call(block_kernel, out_shape=[jax.ShapeDtypeStruct((TOK, D), bf...]
    pallas_call x0 -> x1, Pallas kernels: none -> 3.39 us  [combine(): pl.pallas_call(combine_kernel, grid=(4,), out_shape=[shape, shape], in_sp...]
    unnamed x3 -> x7, local copies, waits for them, and re-layouts: 8.88 us -> 8.1 us
where the time goes in v5:
time: 321 us
  Pallas kernels  312 us (97%)
  local copies, waits for them, and re-layouts  8.1 us (3%)
    pallas_call x1, Pallas kernels, block(): pl.pallas_call(block_kernel, out_shape=[jax.ShapeDtypeStruct((TOK, D), bf...  309 us
    unnamed x7, local copies, waits for them, and re-layouts  8.1 us

profile of v5, /device:TPU:1, one launch (start us, length us, event | category | flops | bytes accessed | tf_op | source)
XLA Modules:
  0.0 320.7 jit_solution(10620559457579097562)
XLA Ops:
  0.6 4.3 %copy.9 = bf16[64,8,2,1536]{3,1,2,0:T(8,128)(2,1)} copy(bf16[64,8,2,1536]{3,2,1,0:T(2,128)(2,1)} %bitcast.15) | data formatting | bytes 6291456
  4.9 308.6 %block.1 = (bf16[128,4096]{1,0:T(8,128)(2,1)}, bf16[128,9,8,128]{3,2,1,0:T(8,128)(2,1)}, bf16[256,288]{1,0:T(8,128)(2,1)}) custom-call(bf16[128,4096]{1,0:T(8,128)(2,1)} %bitcast.18, bf16[128,512]{1,0:T(8,128)(2,1)} %bitcast.21, f32[1,4096]{1,0:T(1,128)} %bitcast.22, s32[8,128]{1,0:T(8,128)} %bitcast.23, f32[8,128]{1,0:T(8,128)} %bitcast.24, ...), custom_call_target="tpu_custom_call" | custom-call | flops 25999998976 | bytes 12582912 | tf_op jit(solution)/shard_map/block/pallas_call | solution.py:443
  313.5 0.0 copy-start
  313.5 1.7 copy-done
  315.2 0.0 copy-start.1
  315.2 1.2 copy-done.1
  316.4 0.0 copy-start.2
  316.4 0.9 copy-done.2
  317.3 3.4 %combine.1 = (bf16[128,4096]{1,0:T(8,128)(2,1)}, bf16[128,4096]{1,0:T(8,128)(2,1)}) custom-call(bf16[128,9,8,128]{3,2,1,0:T(8,128)(2,1)S(1)} %copy-done, bf16[256,288]{1,0:T(8,128)(2,1)S(1)} %copy-done.2, bf16[128,4096]{1,0:T(8,128)(2,1)S(1)} %copy-done.1), custom_call_target="tpu_custom_call" | custom-call | tf_op jit(solution)/shard_map/combine/pallas_call | solution.py:500
Async XLA Ops:
  313.5 1.7 copy-start
  315.2 1.2 copy-start.1
  316.4 0.9 copy-start.2
